TPU v7x, 32 devices: a whole 2x2x4 slice. The times are simulated.
32 devices in a mesh: groups: 2 (over y), row: 8 (over z, x), col: 2 (over core).
Axes of the slice: x: 2, y: 2, z: 4, core: 2. Of those that a mesh axis runs over, the one named last changes fastest.
Arguments:
- object_slices: float32 [4, 2, 2048, 512], P(None, None, ('groups', 'row'), 'col'), parts along dimension 2, may hold values from -4 to 4
- probe: float32 [16, 2, 128, 128], P('groups'), parts along dimension 0, may hold values from -3 to 3
- taps: float32 [2, 63], replicated, may hold values from -0.5 to 0.5
- measured: float32 [64, 128, 128], P(('groups', 'row', 'col')), parts along dimension 0, may hold values from 0.5 to 16
- positions: int32 [64, 2], P(('groups', 'row', 'col')), parts along dimension 0, may hold values from -64 to 959, as said below
Outputs:
- object_grad: float32 [4, 2, 2048, 512], P(None, None, ('groups', 'row'), 'col'), parts along dimension 2
- new_probe: float32 [16, 2, 16384], P('groups', None, ('row', 'col')), parts along dimension 0
There are 2 independent parts, one for each index of `groups`. A program takes and returns all parts, laid end to end along the dimension named above; an argument that names none is the same for every part. Nothing has to cross between parts.
Inputs may be any that keep to these rules, and one draw needn't show every extreme that they name: `positions`: record r belongs to device d = r // 2 in row-major order over the (row, col) device grid, with tile indices (i, q); its row lies in [i * 128 - 128/2, (i + 1) * 128 - 128/2) and its column in [q * 256 - 128/2, (q + 1) * 256 - 128/2).
All inputs are finite; a program needn't handle non-finite values.
Results may differ from a plain program's by a relative error of at most 0.0003.
Values sent between devices are 32-bit elements; how exact they have to be, the bound alone decides.
A program may use at most 64 MiB of HBM per device.

v0:
```python
import math

import jax
import jax.numpy as jnp
from jax import lax
from jax.sharding import PartitionSpec as P

highest_mode = lax.Precision.HIGHEST


def from_behind(value, axis, steps):
    count = lax.axis_size(axis)
    first, last = (max(0, -steps), min(count, count - steps))
    return lax.ppermute(value, axis, [(source, source + steps) for source in range(first, last)])


def with_halo(array, sides, width):
    for axis, dim in sides:
        devices, length = (lax.axis_size(axis), array.shape[dim])
        up = [(i, (i + 1) % devices) for i in range(devices - 1)]
        down = [(j, i) for i, j in up]
        last = lax.slice_in_dim(array, length - width, length, axis=dim)
        first = lax.slice_in_dim(array, 0, width, axis=dim)
        before = lax.ppermute(last, axis, up)
        after = lax.ppermute(first, axis, down)
        array = jnp.concatenate([before, array, after], axis=dim)
    return array


def einsum_exact(form, first, second):
    return jnp.einsum(form, first, second, precision=highest_mode)


def make_tables(taps, width):
    reach = taps.shape[1] // 2
    pixel_idx = lax.iota(jnp.int32, width)
    offset = pixel_idx[None, :] - pixel_idx[:, None] + reach
    tap_idx = lax.iota(jnp.int32, taps.shape[1])
    one_hot = (offset[:, :, None] == tap_idx[None, None, :]).astype(jnp.float32)
    band_re = einsum_exact("abt,t->ab", one_hot, taps[0])
    band_im = einsum_exact("abt,t->ab", one_hot, taps[1])
    phase_idx = pixel_idx[:, None] * pixel_idx[None, :] % width
    angle = 2.0 * math.pi / width * phase_idx.astype(jnp.float32)
    norm_factor = 1.0 / math.sqrt(width)
    return (band_re, band_im, jnp.cos(angle) * norm_factor, -jnp.sin(angle) * norm_factor)


def both_sides(mat_re, mat_im, wave_re, wave_im):
    left_re = einsum_exact("ab,kbc->kac", mat_re, wave_re) - einsum_exact(
        "ab,kbc->kac", mat_im, wave_im
    )
    left_im = einsum_exact("ab,kbc->kac", mat_re, wave_im) + einsum_exact(
        "ab,kbc->kac", mat_im, wave_re
    )
    out_re = einsum_exact("kac,dc->kad", left_re, mat_re) - einsum_exact(
        "kac,dc->kad", left_im, mat_im
    )
    out_im = einsum_exact("kac,dc->kad", left_re, mat_im) + einsum_exact(
        "kac,dc->kad", left_im, mat_re
    )
    return (out_re, out_im)


def record_loss(probe, patch, measured_one, tables):
    band_re, band_im, dft_re, dft_im = tables
    wave_re = probe[:, 0]
    wave_im = probe[:, 1]
    layers = patch.shape[0]
    for layer_idx in range(layers):
        obj_re = patch[layer_idx, 0]
        obj_im = patch[layer_idx, 1]
        wave_re, wave_im = (
            wave_re * obj_re - wave_im * obj_im,
            wave_re * obj_im + wave_im * obj_re,
        )
        if layer_idx + 1 < layers:
            wave_re, wave_im = both_sides(band_re, band_im, wave_re, wave_im)
    far_re, far_im = both_sides(dft_re, dft_im, wave_re, wave_im)
    intensity = jnp.sum(far_re * far_re + far_im * far_im, axis=0)
    weight = 1.0 / (8.0 * probe.shape[0])
    return 0.5 * weight * jnp.sum((intensity - measured_one) ** 2)


def accumulate(grid, probe, measured, places, tables, patch_width):
    sizes = (grid.shape[0], 2, patch_width, patch_width)

    def one_record(carry, item):
        grad_grid, grad_probe = carry
        place, measured_one = item
        zero_idx = jnp.zeros((), jnp.int32)
        starts = (zero_idx, zero_idx, place[0], place[1])
        patch = lax.dynamic_slice(grid, starts, sizes)
        grad_wave, grad_patch = jax.grad(record_loss, argnums=(0, 1))(
            probe, patch, measured_one, tables
        )
        current = lax.dynamic_slice(grad_grid, starts, sizes)
        grad_grid = lax.dynamic_update_slice(grad_grid, current + grad_patch, starts)
        return ((grad_grid, grad_probe + grad_wave), None)

    init = (jnp.zeros(grid.shape, jnp.float32), jnp.zeros(probe.shape, jnp.float32))
    (grad_grid, grad_probe), unused = lax.scan(one_record, init, (places, measured))
    return (grad_grid, grad_probe)


def gram_of(first, second):
    stacked = jnp.concatenate([first, second], axis=0)
    col_re = stacked[:, 0]
    col_im = stacked[:, 1]
    gram_re = einsum_exact("ax,bx->ab", col_re, col_re) + einsum_exact("ax,bx->ab", col_im, col_im)
    gram_im = einsum_exact("ax,bx->ab", col_re, col_im) - einsum_exact("ax,bx->ab", col_im, col_re)
    return (gram_re, gram_im)


def complex_cholesky(herm_re, herm_im):
    count = herm_re.shape[0]
    order_idx = lax.iota(jnp.int32, count)
    cols_re = []
    cols_im = []
    for col_idx in range(count):
        numer_re = herm_re[:, col_idx]
        numer_im = herm_im[:, col_idx]
        for prev_idx in range(col_idx):
            vec_re = cols_re[prev_idx]
            vec_im = cols_im[prev_idx]
            pivot_re = vec_re[col_idx]
            pivot_im = vec_im[col_idx]
            numer_re = numer_re - (vec_re * pivot_re + vec_im * pivot_im)
            numer_im = numer_im - (vec_im * pivot_re - vec_re * pivot_im)
        diag_val = jnp.sqrt(numer_re[col_idx])
        below = order_idx > col_idx
        at_diag = order_idx == col_idx
        cols_re.append(
            jnp.where(below, numer_re / diag_val, 0.0) + jnp.where(at_diag, diag_val, 0.0)
        )
        cols_im.append(jnp.where(below, numer_im / diag_val, 0.0))
    return (jnp.stack(cols_re, axis=1), jnp.stack(cols_im, axis=1))


def lower_inverse(low_re, low_im):
    count = low_re.shape[0]
    unit = jnp.eye(count, dtype=low_re.dtype)
    rows_re = []
    rows_im = []
    for row_idx in range(count):
        acc_re = unit[row_idx]
        acc_im = jnp.zeros_like(unit[row_idx])
        for prev_idx in range(row_idx):
            coef_re = low_re[row_idx, prev_idx]
            coef_im = low_im[row_idx, prev_idx]
            acc_re = acc_re - (coef_re * rows_re[prev_idx] - coef_im * rows_im[prev_idx])
            acc_im = acc_im - (coef_re * rows_im[prev_idx] + coef_im * rows_re[prev_idx])
        rows_re.append(acc_re / low_re[row_idx, row_idx])
        rows_im.append(acc_im / low_re[row_idx, row_idx])
    return (jnp.stack(rows_re, axis=0), jnp.stack(rows_im, axis=0))


def orthonormalize(probe_cols, grad_cols, gram_re, gram_im, scale_out):
    modes = probe_cols.shape[0]
    trace_pp = jnp.trace(gram_re[:modes, :modes])
    trace_gg = jnp.trace(gram_re[modes:, modes:])
    factor = 0.5 * jnp.sqrt(trace_pp / (trace_gg + 1e-06))
    new_re = (
        gram_re[:modes, :modes]
        - factor * (gram_re[:modes, modes:] + gram_re[modes:, :modes])
        + factor * factor * gram_re[modes:, modes:]
    )
    new_im = (
        gram_im[:modes, :modes]
        - factor * (gram_im[:modes, modes:] + gram_im[modes:, :modes])
        + factor * factor * gram_im[modes:, modes:]
    )
    low_re, low_im = complex_cholesky(new_re, new_im)
    inv_re, inv_im = lower_inverse(low_re, low_im)
    right_re = inv_re.T
    right_im = -inv_im.T
    moved = probe_cols - factor * grad_cols
    moved_re = moved[:, 0]
    moved_im = moved[:, 1]
    out_re = einsum_exact("kx,kj->jx", moved_re, right_re) - einsum_exact(
        "kx,kj->jx", moved_im, right_im
    )
    out_im = einsum_exact("kx,kj->jx", moved_re, right_im) + einsum_exact(
        "kx,kj->jx", moved_im, right_re
    )
    return jnp.stack([out_re, out_im], axis=1) * scale_out


def fold_axis(grad, dim, half):
    full = grad.shape[dim]
    inner = full - 2 * half
    core = lax.slice_in_dim(grad, half, half + inner, axis=dim)
    for step_by in (1, -1):
        if step_by == 1:
            sent = lax.slice_in_dim(grad, half + inner, full, axis=dim)
        else:
            sent = lax.slice_in_dim(grad, 0, half, axis=dim)
        if dim == 2:
            arrived = from_behind(sent, "row", step_by)
        else:
            arrived = from_behind(sent, "col", step_by)
        widths = [(0, 0)] * grad.ndim
        if step_by == 1:
            widths[dim] = (0, inner - half)
        else:
            widths[dim] = (inner - half, 0)
        core = core + jnp.pad(arrived, widths)
    return core


def per_device(object_slices, probe, taps, measured, positions):
    width = probe.shape[-1]
    half = width // 2
    tile_rows = object_slices.shape[2]
    tile_cols = object_slices.shape[3]
    tables = make_tables(taps, width)
    extended = with_halo(object_slices, (("row", 2), ("col", 3)), half)
    anchor = jnp.stack(
        [lax.axis_index("row") * tile_rows - half, lax.axis_index("col") * tile_cols - half]
    )
    places = positions - anchor[None, :]
    grad_ext, grad_probe = accumulate(extended, probe, measured, places, tables, width)
    folded = fold_axis(fold_axis(grad_ext, 2, half), 3, half)
    modes = probe.shape[0]
    pixels = width * width
    probe_cols = probe.reshape(modes, 2, pixels)
    grad_cols = grad_probe.reshape(modes, 2, pixels)
    share = pixels // (lax.axis_size("row") * lax.axis_size("col"))
    start = lax.axis_index(("row", "col")) * share
    own_probe = lax.dynamic_slice_in_dim(probe_cols, start, share, 2)
    total_grad = lax.psum(grad_cols, ("row", "col"))
    gram_re, gram_im = gram_of(probe_cols, total_grad)
    own_grad = lax.dynamic_slice_in_dim(total_grad, start, share, 2)
    new_probe = orthonormalize(own_probe, own_grad, gram_re, gram_im, float(width))
    return (folded, new_probe)


def solution(mesh):
    placed = (
        P(None, None, ("groups", "row"), "col"),
        P("groups", None, None, None),
        P(),
        P(("groups", "row", "col"), None, None),
        P(("groups", "row", "col"), None),
    )
    return jax.shard_map(
        per_device,
        mesh=mesh,
        in_specs=placed,
        out_specs=(P(None, None, ("groups", "row"), "col"), P("groups", None, ("row", "col"))),
        check_vma=False,
    )
```

profile of v0, /device:TPU:0, one launch (start us, length us, event | category | flops | bytes accessed | tf_op | source)
XLA Modules:
  0.0 651.2 jit_solution(16764180511014686650)
XLA Ops:
  8.5 4.9 collective-permute-start
  18.0 17.8 %collective-permute-done = f32[4,2,64,256]{3,2,1,0:T(8,128)S(1)} collective-permute-done((f32[4,2,64,256]{3,2,1,0:T(8,128)S(1)}, f32[4,2,64,256]{3,2,1,0:T(8,128)S(1)}, u32[]{:S(2)}, u32[]{:S(2)}) %collective-permute-start) | collective-permute-done | bytes 524320 | tf_op jit(solution)/shard_map/ppermute | solution.py:24
  44.0 3.3 fusion.235
  47.3 3.2 fusion.233
  50.5 3.8 pad_maximum_fusion
  56.2 173.3 %while.16 = (s32[]{:T(128)}, f32[4,2,256,384]{3,2,1,0:T(8,128)}, f32[8,2,128,128]{2,3,0,1:T(8,128)}, s32[2,2]{1,0:T(2,128)S(1)}, f32[8,2,128,128]{2,3,0,1:T(8,12...) while((s32[]{:T(128)}, f32[4,2,256,384]{3,2,1,0:T(8,128)}, ...), condition=%wide.region_18.19_spmd.clone.clone, body=%wide.region_0.18_spmd.clone.clone.sunk | while | flops 12914802688 | bytes 137233312 | solution.py:101
  90.1 2.5 fusion.624
  130.8 7.7 %dynamic_update_slice.9 = f32[4,2,256,384]{3,2,1,0:T(8,128)} dynamic-update-slice(f32[4,2,256,384]{3,2,1,0:T(8,128)} %get-tuple-element.615, f32[4,2,128,128]{3,2,1,0:T(8,128)S(1)} %add_add_fusion.2, s32[]{:T(128)} %constant.94.clone.1..sunk, s32[]{:T(128)} %constant.94.clone.1..sunk, s32[]{:T(128)S(6)} %select_n.471, s32[]{:T(128)S(6)} %select_n.472) | dynamic-update-slice | bytes 1048580 | tf_op jit(solution)/shard_map/while/body/eval_jaxpr/dynamic_update_slice | solution.py:97
  214.8 7.2 %dynamic_update_slice.9 = f32[4,2,256,384]{3,2,1,0:T(8,128)} dynamic-update-slice(f32[4,2,256,384]{3,2,1,0:T(8,128)} %get-tuple-element.615, f32[4,2,128,128]{3,2,1,0:T(8,128)S(1)} %add_add_fusion.2, s32[]{:T(128)} %constant.94.clone.1..sunk, s32[]{:T(128)} %constant.94.clone.1..sunk, s32[]{:T(128)S(6)} %select_n.471, s32[]{:T(128)S(6)} %select_n.472) | dynamic-update-slice | bytes 1048580 | tf_op jit(solution)/shard_map/while/body/eval_jaxpr/dynamic_update_slice | solution.py:97
  233.0 2.7 fusion.298
  235.7 4.7 collective-permute-start.4
  241.7 91.7 %all-reduce.16.cloned.1.call-done = f32[8,2,16384]{2,0,1:T(8,128)} async-done(((f32[8,2,16384]{2,0,1:T(8,128)}), f32[8,2,16384]{2,0,1:T(8,128)}) %all-reduce.16.cloned.1.call-update) | async-done | bytes 1048592 | tf_op jit(solution)/shard_map/psum | solution.py:230
  333.4 2.7 fusion.295
  336.1 2.7 convolution_add_fusion.25
  363.1 3.8 fusion.286
  368.2 3.8 compare_select_fusion.15
  374.8 5.0 fusion.282
  381.1 5.1 compare_select_fusion.13
  388.9 6.2 add_subtract_fusion.2
  396.3 6.2 compare_select_fusion.11
  405.0 7.6 %add_subtract_fusion.1 = f32[8]{0:T(128)S(1)} fusion(f32[8]{0:T(128)S(1)} %compare_select_fusion.11, f32[8]{0:T(128)S(1)} %compare_select_fusion.13, f32[8]{0:T(128)S(1)} %compare_select_fusion.15, f32[8]{0:T(128)S(1)} %compare_select_fusion.17, f32[8]{0:T(128)S(1)} %compare_select_fusion.19, f32[8]{0:T(128)S(1)} %get-tuple-element.459, ...), kind=kLoop, calls=%fused_computation.455 | loop fusion | flops 432 | bytes 516 | tf_op jit(solution)/shard_map/sub | solution.py:127
  413.9 7.6 %compare_select_fusion.9 = f32[8]{0:T(128)S(1)} fusion(f32[8]{0:T(128)S(1)} %compare_select_fusion.11, f32[8]{0:T(128)S(1)} %compare_select_fusion.13, f32[8]{0:T(128)S(1)} %compare_select_fusion.15, f32[8]{0:T(128)S(1)} %compare_select_fusion.17, f32[8]{0:T(128)S(1)} %compare_select_fusion.19, f32[8]{0:T(128)S(1)} %get-tuple-element.460, ...), kind=kLoop, calls=%fused_computation.391 | loop fusion | flops 456 | bytes 520 | tf_op jit(solution)/shard_map/jit(_where)/select_n | solution.py:135
  423.3 8.8 %add_subtract_fusion = f32[8]{0:T(128)S(1)} fusion(f32[8]{0:T(128)S(1)} %compare_select_fusion.9, f32[8]{0:T(128)S(1)} %compare_select_fusion.11, f32[8]{0:T(128)S(1)} %compare_select_fusion.13, f32[8]{0:T(128)S(1)} %compare_select_fusion.15, f32[8]{0:T(128)S(1)} %compare_select_fusion.17, f32[8]{0:T(128)S(1)} %compare_select_fusion.19, ...), kind=kLoop, calls=%fused_computation.454 | loop fusion | flops 512 | bytes 592 | tf_op jit(solution)/shard_map/sub | solution.py:127
  433.8 39.2 %subtract_divide_fusion.1 = (f32[1,8]{0,1:T(8,128)S(1)}, f32[1,8]{0,1:T(8,128)S(1)}, f32[1,8]{0,1:T(8,128)S(1)}, f32[1,8]{0,1:T(8,128)S(1)}, f32[1,8]{0,1:T(8,128)S(1)}) fusion(f32[8,8]{0,1:T(8,128)S(1)} %fusion.251, f32[]{:T(128)} %bitcast.99, f32[]{:T(128)} %bitcast.67, f32[]{:T(128)S(6)} %mul.2504, f32[]{:T(128)} %bitcast.96, f32[]{:T(128)} %bitcast.94, ...), kind=kLoop, calls=%fused_computation.360 | loop fusion | flops 1576 | bytes 720 | tf_op jit(solution)/shard_map/div | solution.py:152
  473.0 27.4 %subtract_divide_fusion.3 = f32[1,8]{0,1:T(8,128)S(1)} fusion(f32[]{:T(128)} %bitcast.81, f32[1,8]{0,1:T(8,128)S(1)} %get-tuple-element.353, f32[1,8]{0,1:T(8,128)S(1)} %get-tuple-element.354, f32[1,8]{0,1:T(8,128)S(1)} %get-tuple-element.355, f32[1,8]{0,1:T(8,128)S(1)} %get-tuple-element.356, f32[]{:T(128)} %bitcast.53, f32[8,8]{0,1:T(8,128)S(1)} %fusion.251, ...), kind=kLoop, calls=%fused_computation.362 | loop fusion | flops 960 | bytes 464 | tf_op jit(solution)/shard_map/div | solution.py:152
  500.4 19.0 %subtract_divide_fusion.5 = f32[1,8]{0,1:T(8,128)S(1)} fusion(f32[1,8]{0,1:T(8,128)S(1)} %get-tuple-element.354, f32[1,8]{0,1:T(8,128)S(1)} %get-tuple-element.355, f32[1,8]{0,1:T(8,128)S(1)} %get-tuple-element.356, f32[1,8]{0,1:T(8,128)S(1)} %get-tuple-element.353, f32[8,8]{0,1:T(8,128)S(1)} %fusion.251, f32[]{:T(128)} %bitcast.65, f32[]{:T(128)} %bitcast.41, ...), kind=kLoop, calls=%fused_computation.365 | loop fusion | flops 608 | bytes 372 | tf_op jit(solution)/shard_map/div | solution.py:152
  519.4 12.3 %subtract_divide_fusion.7 = f32[1,8]{0,1:T(8,128)S(1)} fusion(f32[1,8]{0,1:T(8,128)S(1)} %get-tuple-element.353, f32[1,8]{0,1:T(8,128)S(1)} %get-tuple-element.354, f32[1,8]{0,1:T(8,128)S(1)} %get-tuple-element.355, f32[1,8]{0,1:T(8,128)S(1)} %get-tuple-element.356, f32[8,8]{0,1:T(8,128)S(1)} %fusion.251, f32[]{:T(128)} %bitcast.51, f32[]{:T(128)} %bitcast.31, ...), kind=kLoop, calls=%fused_computation.368 | loop fusion | flops 320 | bytes 288 | tf_op jit(solution)/shard_map/div | solution.py:152
  532.3 27.3 %subtract_divide_fusion.2 = f32[1,8]{0,1:T(8,128)S(1)} fusion(f32[1,8]{0,1:T(8,128)S(1)} %get-tuple-element.353, f32[1,8]{0,1:T(8,128)S(1)} %get-tuple-element.354, f32[1,8]{0,1:T(8,128)S(1)} %get-tuple-element.355, f32[1,8]{0,1:T(8,128)S(1)} %get-tuple-element.356, f32[]{:T(128)} %bitcast.67, f32[]{:T(128)S(6)} %mul.2504, f32[]{:T(128)} %bitcast.81, ...), kind=kLoop, calls=%fused_computation.361 | loop fusion | flops 960 | bytes 432 | tf_op jit(solution)/shard_map/div | solution.py:153
  559.6 19.0 %subtract_divide_fusion.4 = f32[1,8]{0,1:T(8,128)S(1)} fusion(f32[1,8]{0,1:T(8,128)S(1)} %get-tuple-element.353, f32[1,8]{0,1:T(8,128)S(1)} %get-tuple-element.354, f32[1,8]{0,1:T(8,128)S(1)} %get-tuple-element.355, f32[1,8]{0,1:T(8,128)S(1)} %get-tuple-element.356, f32[]{:T(128)} %bitcast.53, f32[]{:T(128)S(6)} %mul.2430, f32[]{:T(128)} %bitcast.65, ...), kind=kLoop, calls=%fused_computation.363 | loop fusion | flops 608 | bytes 340 | tf_op jit(solution)/shard_map/div | solution.py:153
  578.6 7.2 %subtract_divide_fusion.8 = (f32[1,8]{0,1:T(8,128)S(1)}, f32[1,8]{0,1:T(8,128)S(1)}, f32[1,8]{0,1:T(8,128)S(1)}) fusion(f32[1,8]{0,1:T(8,128)S(1)} %get-tuple-element.354, f32[1,8]{0,1:T(8,128)S(1)} %get-tuple-element.355, f32[1,8]{0,1:T(8,128)S(1)} %get-tuple-element.356, f32[]{:T(128)} %bitcast.31, f32[]{:T(128)S(6)} %mul.2318, f32[]{:T(128)} %bitcast.39, ...), kind=kLoop, calls=%fused_computation.369 | loop fusion | flops 192 | bytes 252 | tf_op jit(solution)/shard_map/div | solution.py:153
  585.8 36.6 %subtract_divide_fusion = f32[1,8]{0,1:T(8,128)S(1)} fusion(f32[1,8]{0,1:T(8,128)S(1)} %get-tuple-element.353, f32[1,8]{0,1:T(8,128)S(1)} %get-tuple-element.354, f32[1,8]{0,1:T(8,128)S(1)} %get-tuple-element.355, f32[1,8]{0,1:T(8,128)S(1)} %get-tuple-element.356, f32[]{:T(128)} %bitcast.83, f32[]{:T(128)S(6)} %mul.2550, f32[]{:T(128)} %bitcast.99, ...), kind=kLoop, calls=%fused_computation.359 | loop fusion | flops 1376 | bytes 532 | tf_op jit(solution)/shard_map/div | solution.py:153
  622.5 12.2 %subtract_divide_fusion.6 = f32[1,8]{0,1:T(8,128)S(1)} fusion(f32[1,8]{0,1:T(8,128)S(1)} %get-tuple-element.353, f32[1,8]{0,1:T(8,128)S(1)} %get-tuple-element.354, f32[1,8]{0,1:T(8,128)S(1)} %get-tuple-element.355, f32[1,8]{0,1:T(8,128)S(1)} %get-tuple-element.356, f32[]{:T(128)} %bitcast.41, f32[]{:T(128)S(6)} %mul.2368, f32[]{:T(128)} %bitcast.51, ...), kind=kLoop, calls=%fused_computation.366 | loop fusion | flops 320 | bytes 256 | tf_op jit(solution)/shard_map/div | solution.py:153
  (339 shorter events, 193.5 us)
Async XLA Ops:
  7.2 326.2 %all-reduce.16.cloned.1.call-start = ((), (), s32[]{:S(2)}) async-start(), calls=%async_computation | async-start | bytes 2097152 | tf_op jit(solution)/shard_map/psum | solution.py:230
  8.5 27.2 %collective-permute-start = (f32[4,2,64,256]{3,2,1,0:T(8,128)S(1)}, f32[4,2,64,256]{3,2,1,0:T(8,128)S(1)}, u32[]{:S(2)}, u32[]{:S(2)}) collective-permute-start(f32[4,2,64,256]{3,2,1,0:T(8,128)S(1)} %get-tuple-element.392), channel_id=1, source_target_pairs={{0,2},{2,4},{4,6},{6,8},{8,10},{10,12},{12,14},{1,3},{3,5},{5,7},{... | collective-permute-start | bytes 1572872 | tf_op jit(solution)/shard_map/ppermute | solution.py:24
  13.4 22.7 %collective-permute-start.1 = (f32[4,2,64,256]{3,2,1,0:T(8,128)S(1)}, f32[4,2,64,256]{3,2,1,0:T(8,128)}, u32[]{:S(2)}, u32[]{:S(2)}) collective-permute-start(f32[4,2,64,256]{3,2,1,0:T(8,128)S(1)} %get-tuple-element.393), channel_id=1, source_target_pairs={{2,0},{4,2},{6,4},{8,6},{10,8},{12,10},{14,12},{3,1},{5,3},{7,5},{... | collective-permute-start | bytes 1572872 | tf_op jit(solution)/shard_map/ppermute | solution.py:25
  36.1 6.2 copy-start.23
  37.5 4.9 copy-start.9
  37.5 6.4 copy-start.24
  39.0 11.5 %collective-permute-start.2 = (f32[4,2,256,64]{2,3,1,0:T(8,128)}, f32[4,2,256,64]{2,3,1,0:T(8,128)}, u32[]{:S(2)}, u32[]{:S(2)}) collective-permute-start(f32[4,2,256,64]{2,3,1,0:T(8,128)} %get-tuple-element.388), channel_id=1, source_target_pairs={{0,1},{2,3},{4,5},{6,7},{8,9},{10,11},{12,13},{14,15},{16,17},{18,... | collective-permute-start | bytes 1572872 | tf_op jit(solution)/shard_map/ppermute | solution.py:24
  41.1 9.5 %collective-permute-start.3 = (f32[4,2,256,64]{2,3,1,0:T(8,128)}, f32[4,2,256,64]{2,3,1,0:T(8,128)}, u32[]{:S(2)}, u32[]{:S(2)}) collective-permute-start(f32[4,2,256,64]{2,3,1,0:T(8,128)} %get-tuple-element.389), channel_id=1, source_target_pairs={{1,0},{3,2},{5,4},{7,6},{9,8},{11,10},{13,12},{15,14},{17,16},{19,... | collective-permute-start | bytes 1572872 | tf_op jit(solution)/shard_map/ppermute | solution.py:25
  44.0 6.6 %copy-start.10 = (f32[4,2,64,256]{2,3,1,0:T(8,128)S(1)}, f32[4,2,64,256]{2,3,1,0:T(8,128)}, u32[]{:S(2)}) copy-start(f32[4,2,64,256]{2,3,1,0:T(8,128)} %copy-done.9) | copy-start | bytes 1572868
  56.2 9.2 %copy-start = (f32[8,2,128,128]{2,3,0,1:T(8,128)}, f32[8,2,128,128]{2,3,0,1:T(8,128)S(1)}, u32[]{:S(2)}) copy-start(f32[8,2,128,128]{2,3,0,1:T(8,128)S(1)} %get-tuple-element.634) | copy-start | bytes 3145732 | tf_op jit(solution)/shard_map/while
  63.1 3.4 copy-start.6
  90.1 4.6 copy-start.2
  90.1 4.6 copy-start.3
  97.2 4.6 copy-start.22
  122.8 3.6 copy-start.5
  122.8 3.6 copy-start.7
  138.9 9.2 %copy-start = (f32[8,2,128,128]{2,3,0,1:T(8,128)}, f32[8,2,128,128]{2,3,0,1:T(8,128)S(1)}, u32[]{:S(2)}) copy-start(f32[8,2,128,128]{2,3,0,1:T(8,128)S(1)} %get-tuple-element.634) | copy-start | bytes 3145732 | tf_op jit(solution)/shard_map/while
  145.8 3.4 copy-start.6
  172.8 4.4 copy-start.2
  172.8 4.4 copy-start.3
  179.6 4.5 copy-start.22
  205.4 3.6 copy-start.5
  205.4 3.6 copy-start.7
  209.1 3.7 copy-start.11
  209.1 3.7 copy-start.12
  209.1 3.7 copy-start.13
  209.1 3.7 copy-start.14
  235.7 399.6 %collective-permute-start.4 = (f32[4,2,64,384]{3,2,1,0:T(8,128)}, f32[4,2,64,384]{3,2,1,0:T(8,128)S(1)}, u32[]{:S(2)}, u32[]{:S(2)}) collective-permute-start(f32[4,2,64,384]{3,2,1,0:T(8,128)} %get-tuple-element.386), channel_id=1, source_target_pairs={{0,2},{2,4},{4,6},{6,8},{8,10},{10,12},{12,14},{1,3},{3,5},{5,7},{... | collective-permute-start | bytes 2359304 | tf_op jit(solution)/shard_map/ppermute | solution.py:14
  240.4 394.9 %collective-permute-start.5 = (f32[4,2,64,384]{3,2,1,0:T(8,128)}, f32[4,2,64,384]{3,2,1,0:T(8,128)}, u32[]{:S(2)}, u32[]{:S(2)}) collective-permute-start(f32[4,2,64,384]{3,2,1,0:T(8,128)} %get-tuple-element.387), channel_id=1, source_target_pairs={{2,0},{4,2},{6,4},{8,6},{10,8},{12,10},{14,12},{3,1},{5,3},{7,5},{... | collective-permute-start | bytes 2359304 | tf_op jit(solution)/shard_map/ppermute | solution.py:14
  333.4 8.8 %copy-start.8 = (f32[8,2,16384]{2,0,1:T(8,128)S(1)}, f32[8,2,16384]{2,0,1:T(8,128)}, u32[]{:S(2)}) copy-start(f32[8,2,16384]{2,0,1:T(8,128)} %all-reduce.16.cloned.1.call-done) | copy-start | bytes 3145732
  637.3 3.8 collective-permute-start.6
  638.7 3.8 collective-permute-start.7
  (21 other events, 47.2 us)
Sparse Core Ops, SparseCore 0:
  232.5 100.8 all-reduce.15
where the time goes:
time: 663 us; the launch traced here: 651 us
  other arithmetic  279 us (42%)
  matrix products  135 us (20%)
  waiting for transfers between devices  111 us (17%)
  local copies, waits for them, and re-layouts  59.8 us (9%)
  between operations  31.1 us (5%)
  starting transfers between devices  18.1 us (3%)
  loops' own time  17.6 us (3%)
    dot_general x138, matrix products, einsum_exact(): return jnp.einsum(form, first, second, precision=highest_mode)  135 us
    div x5, other arithmetic, lower_inverse(): rows_im.append(acc_im / low_re[row_idx, row_idx])  102 us
    div x4, other arithmetic, lower_inverse(): rows_re.append(acc_re / low_re[row_idx, row_idx])  97.9 us
    psum x1, waiting for transfers between devices, per_device(): total_grad = lax.psum(grad_cols, ('row', 'col'))  91.7 us
    sub x7, other arithmetic, complex_cholesky(): numer_re = numer_re - (vec_re * pivot_re + vec_im * pivot_im)  34.9 us
    select_n x7, other arithmetic, complex_cholesky(): cols_im.append(jnp.where(below, numer_im / diag_val, 0.0))  26.1 us
    ppermute x2, waiting for transfers between devices, with_halo(): before = lax.ppermute(last, axis, up)  17.8 us
    another operation x1, loops' own time, accumulate(): lax.scan(one_record, init, (places, measured))  17.6 us
  transfers between devices with their start and end apart: 9, of which 3 were waited for; matrix products, arithmetic and copies ran while one was open for 46% of the time, Pallas kernels for 0%

commit v1 on v0

v1 whole, which is shorter than its diff:
```python
import functools
import math

import jax
import jax.numpy as jnp
import numpy as np
from jax import lax
from jax.experimental import pallas as pl
from jax.experimental.pallas import tpu as pltpu
from jax.sharding import PartitionSpec as P

highest_mode = lax.Precision.HIGHEST
EDGE = 128


def split(value):
    high = value.astype(jnp.bfloat16)
    low = (value - high.astype(jnp.float32)).astype(jnp.bfloat16)
    return high, low


def block_matrix(mat_re, mat_im):
    top = jnp.concatenate([mat_re, -mat_im], axis=1)
    bottom = jnp.concatenate([mat_im, mat_re], axis=1)
    return jnp.concatenate([top, bottom], axis=0)


def store_matrices(mat_re, mat_im, trans_re, trans_im, slot, rights, lefts):
    plain = split(block_matrix(mat_re, mat_im))
    turned = split(block_matrix(trans_re, -trans_im))
    for place, (right, left) in ((slot, (turned, plain)), (slot + 2, (plain, turned))):
        rights[place] = jnp.concatenate([right[0], right[0], right[1]], axis=0)
        lefts[place] = jnp.concatenate([left[0], left[0], left[1]], axis=1)


def both_sides(waves, right, left):
    width = waves[0][0].shape[0]
    rows = jnp.concatenate([jnp.concatenate([re, im], axis=1) for re, im in waves], axis=0)
    high, low = split(rows)
    mid = jnp.dot(
        jnp.concatenate([high, low, high], axis=1), right, preferred_element_type=jnp.float32
    )
    parts = []
    for idx in range(len(waves)):
        part = mid[idx * width : (idx + 1) * width]
        parts.append(jnp.concatenate([part[:, :width], part[:, width:]], axis=0))
    cols = jnp.concatenate(parts, axis=1)
    high, low = split(cols)
    out = jnp.dot(
        left, jnp.concatenate([high, low, high], axis=0), preferred_element_type=jnp.float32
    )
    result = []
    for idx in range(len(waves)):
        part = out[:, idx * width : (idx + 1) * width]
        result.append((part[:width], part[width:]))
    return result


def wave_kernel(
    places, taps, ext, probe, measured, dft, gext, gprobe,
    rights, lefts, waves, far, patch, gpatch, level,
):
    modes, _, width, _ = probe.shape
    layers = ext.shape[0]
    records = measured.shape[0]
    count = taps.shape[1]
    reach = count // 2
    group = 4
    weight = 1.0 / (8.0 * modes)

    shape = (width, width)
    offset = lax.broadcasted_iota(jnp.int32, shape, 1) - lax.broadcasted_iota(jnp.int32, shape, 0)
    bands = [jnp.zeros(shape, jnp.float32) for _ in range(4)]
    for idx in range(count):
        ahead = offset == idx - reach
        behind = offset == reach - idx
        bands[0] = jnp.where(ahead, taps[0, idx], bands[0])
        bands[1] = jnp.where(ahead, taps[1, idx], bands[1])
        bands[2] = jnp.where(behind, taps[0, idx], bands[2])
        bands[3] = jnp.where(behind, taps[1, idx], bands[3])
    store_matrices(*bands, 0, rights, lefts)
    store_matrices(dft[0], dft[1], dft[0], dft[1], 1, rights, lefts)
    gext[...] = jnp.zeros_like(gext)
    gprobe[...] = jnp.zeros_like(gprobe)

    def one_record(rec, carry):
        row = places[rec, 0]
        col = places[rec, 1]
        block = pl.multiple_of((col // EDGE) * EDGE, EDGE)
        turn = col - block
        back = lax.rem(2 * EDGE - turn, 2 * EDGE)
        top = pl.multiple_of((row // 8) * 8, 8)
        drop = row - top
        tall = width + 8
        lift = lax.rem(tall - drop, tall)
        for layer in range(layers):
            for part in range(2):
                wide = ext[layer, part, pl.ds(top, tall), pl.ds(block, 2 * EDGE)]
                wide = pltpu.roll(wide, back, 1)[:, :width]
                patch[layer, part] = pltpu.roll(wide, lift, 0)[:width]
        gpatch[...] = jnp.zeros_like(gpatch)
        level[...] = jnp.zeros_like(level)

        def forward(step, carry):
            base = step * group
            now = [(probe[base + k, 0], probe[base + k, 1]) for k in range(group)]
            for layer in range(layers):
                obj_re, obj_im = patch[layer, 0], patch[layer, 1]
                now = [(a * obj_re - b * obj_im, a * obj_im + b * obj_re) for a, b in now]
                slot = 0 if layer + 1 < layers else 1
                now = both_sides(now, rights[slot], lefts[slot])
                for k in range(group):
                    if layer + 1 < layers:
                        waves[layer, base + k, 0] = now[k][0]
                        waves[layer, base + k, 1] = now[k][1]
                    else:
                        far[base + k, 0] = now[k][0]
                        far[base + k, 1] = now[k][1]
            total = level[...]
            for a, b in now:
                total = total + (a * a + b * b)
            level[...] = total
            return carry

        lax.fori_loop(0, modes // group, forward, 0)
        level[...] = (2.0 * weight) * (level[...] - measured[rec])

        def backward(step, carry):
            base = step * group
            scale = level[...]
            now = [(far[base + k, 0] * scale, far[base + k, 1] * scale) for k in range(group)]
            for layer in reversed(range(layers)):
                slot = 2 if layer + 1 < layers else 3
                now = both_sides(now, rights[slot], lefts[slot])
                if layer:
                    before = [
                        (waves[layer - 1, base + k, 0], waves[layer - 1, base + k, 1])
                        for k in range(group)
                    ]
                else:
                    before = [(probe[base + k, 0], probe[base + k, 1]) for k in range(group)]
                sum_re, sum_im = gpatch[layer, 0], gpatch[layer, 1]
                for (a, b), (c, d) in zip(now, before):
                    sum_re = sum_re + (a * c + b * d)
                    sum_im = sum_im + (b * c - a * d)
                gpatch[layer, 0] = sum_re
                gpatch[layer, 1] = sum_im
                obj_re, obj_im = patch[layer, 0], patch[layer, 1]
                now = [(a * obj_re + b * obj_im, b * obj_re - a * obj_im) for a, b in now]
            for k in range(group):
                gprobe[base + k, 0] += now[k][0]
                gprobe[base + k, 1] += now[k][1]
            return carry

        lax.fori_loop(0, modes // group, backward, 0)
        for layer in range(layers):
            for part in range(2):
                wide = jnp.concatenate([gpatch[layer, part], jnp.zeros((8, width), jnp.float32)], axis=0)
                wide = pltpu.roll(wide, drop, 0)
                wide = jnp.concatenate([wide, jnp.zeros((tall, width), jnp.float32)], axis=1)
                where = (layer, part, pl.ds(top, tall), pl.ds(block, 2 * EDGE))
                gext[where] = gext[where] + pltpu.roll(wide, turn, 1)
        return carry

    lax.fori_loop(0, records, one_record, 0)


def run_records(places, taps, ext, probe, measured):
    modes, _, width, _ = probe.shape
    layers = ext.shape[0]
    idx = np.arange(width)
    angle = 2.0 * math.pi / width * (idx[:, None] * idx[None, :] % width)
    dft = np.stack([np.cos(angle), -np.sin(angle)]) / math.sqrt(width)
    smem = pl.BlockSpec(memory_space=pltpu.SMEM)
    vmem = pl.BlockSpec(memory_space=pltpu.VMEM)
    f32 = jnp.float32
    return pl.pallas_call(
        wave_kernel,
        out_shape=(jax.ShapeDtypeStruct(ext.shape, f32), jax.ShapeDtypeStruct(probe.shape, f32)),
        in_specs=[smem, smem, vmem, vmem, vmem, vmem],
        out_specs=(vmem, vmem),
        scratch_shapes=[
            pltpu.VMEM((4, 6 * width, 2 * width), jnp.bfloat16),
            pltpu.VMEM((4, 2 * width, 6 * width), jnp.bfloat16),
            pltpu.VMEM((layers - 1, modes, 2, width, width), f32),
            pltpu.VMEM((modes, 2, width, width), f32),
            pltpu.VMEM((layers, 2, width, width), f32),
            pltpu.VMEM((layers, 2, width, width), f32),
            pltpu.VMEM((width, width), f32),
        ],
        compiler_params=pltpu.CompilerParams(vmem_limit_bytes=48 << 20),
        name="records",
    )(places, taps, ext, probe, measured, jnp.asarray(dft, f32))


def eliminate(gram_re, gram_im, probe_re, probe_im, grad_re, grad_im, scale_out):
    modes = probe_re.shape[0]
    idx = lax.broadcasted_iota(jnp.int32, (modes, modes), 0)
    lane = lax.broadcasted_iota(jnp.int32, (modes, modes), 1)
    diag = idx == lane
    w_pp, w_gg = gram_re[:modes, :modes], gram_re[modes:, modes:]
    trace_pp = jnp.sum(jnp.where(diag, w_pp, 0.0), keepdims=True)
    trace_gg = jnp.sum(jnp.where(diag, w_gg, 0.0), keepdims=True)
    factor = 0.5 * jnp.sqrt(trace_pp / (trace_gg + 1e-06))
    new_re = w_pp - factor * (gram_re[:modes, modes:] + gram_re[modes:, :modes]) + factor * factor * w_gg
    new_im = (
        gram_im[:modes, :modes]
        - factor * (gram_im[:modes, modes:] + gram_im[modes:, :modes])
        + factor * factor * gram_im[modes:, modes:]
    )
    data_re = probe_re - factor * grad_re
    data_im = factor * grad_im - probe_im
    below = lax.broadcasted_iota(jnp.int32, (modes, 1), 0)
    for step in range(modes):
        pivot = new_re[step : step + 1, step : step + 1]
        scale = 1.0 / jnp.sqrt(pivot)
        keep = below > step
        coef_re = jnp.where(keep, new_re[:, step : step + 1] * scale, 0.0)
        coef_im = jnp.where(keep, new_im[:, step : step + 1] * scale, 0.0)
        at = below == step

        def update(re, im):
            row_re = re[step : step + 1] * scale
            row_im = im[step : step + 1] * scale
            next_re = re - (coef_re * row_re - coef_im * row_im)
            next_im = im - (coef_re * row_im + coef_im * row_re)
            return jnp.where(at, row_re, next_re), jnp.where(at, row_im, next_im)

        data_re, data_im = update(data_re, data_im)
        new_re, new_im = update(new_re, new_im)
    return data_re * scale_out, data_im * (-scale_out)


def solve_kernel(scale_out, gram, probe, grad, out):
    out_re, out_im = eliminate(gram[0], gram[1], probe[0], probe[1], grad[0], grad[1], scale_out)
    out[0] = out_re
    out[1] = out_im


def gram_of(first, second):
    stacked = jnp.concatenate([first, second], axis=0)
    both = jnp.concatenate([stacked[:, 0], stacked[:, 1]], axis=0)
    full = jnp.einsum("ax,bx->ab", both, both, precision=highest_mode)
    count = stacked.shape[0]
    return jnp.stack(
        [full[:count, :count] + full[count:, count:], full[:count, count:] - full[count:, :count]]
    )


def with_halo(array, sides):
    for axis, dim, width in sides:
        devices, length = (lax.axis_size(axis), array.shape[dim])
        up = [(i, i + 1) for i in range(devices - 1)]
        down = [(j, i) for i, j in up]
        last = lax.slice_in_dim(array, length - width, length, axis=dim)
        first = lax.slice_in_dim(array, 0, width, axis=dim)
        before = lax.ppermute(last, axis, up)
        after = lax.ppermute(first, axis, down)
        array = jnp.concatenate([before, array, after], axis=dim)
    return array


def fold_axis(grad, axis, dim, half):
    devices, full = lax.axis_size(axis), grad.shape[dim]
    inner = full - 2 * half
    up = [(i, i + 1) for i in range(devices - 1)]
    down = [(j, i) for i, j in up]
    core = lax.slice_in_dim(grad, half, half + inner, axis=dim)
    before = lax.ppermute(lax.slice_in_dim(grad, half + inner, full, axis=dim), axis, up)
    after = lax.ppermute(lax.slice_in_dim(grad, 0, half, axis=dim), axis, down)
    return core + jnp.concatenate([before, after], axis=dim)


def per_device(object_slices, probe, taps, measured, positions):
    modes, _, width, _ = probe.shape
    half = width // 2
    tile_rows = object_slices.shape[2]
    tile_cols = object_slices.shape[3]
    ext = with_halo(object_slices, (("row", 2, half), ("col", 3, EDGE)))
    anchor = jnp.stack(
        [lax.axis_index("row") * tile_rows - half, lax.axis_index("col") * tile_cols - EDGE]
    )
    places = positions - anchor[None, :]
    grad_ext, grad_probe = run_records(places, taps, ext, probe, measured)
    pixels = width * width
    share = pixels // (lax.axis_size("row") * lax.axis_size("col"))
    start = lax.axis_index(("row", "col")) * share
    own_grad = lax.psum_scatter(
        grad_probe.reshape(modes, 2, pixels), ("row", "col"), scatter_dimension=2, tiled=True
    )
    own_probe = lax.dynamic_slice_in_dim(probe.reshape(modes, 2, pixels), start, share, 2)
    gram = lax.psum(gram_of(own_probe, own_grad), ("row", "col"))
    folded = fold_axis(fold_axis(grad_ext, "col", 3, EDGE), "row", 2, half)
    new_probe = pl.pallas_call(
        functools.partial(solve_kernel, float(width)),
        out_shape=jax.ShapeDtypeStruct((2, modes, share), jnp.float32),
        name="solve",
    )(gram, own_probe.transpose(1, 0, 2), own_grad.transpose(1, 0, 2))
    return (folded, new_probe.transpose(1, 0, 2))


def solution(mesh):
    placed = (
        P(None, None, ("groups", "row"), "col"),
        P("groups", None, None, None),
        P(),
        P(("groups", "row", "col"), None, None),
        P(("groups", "row", "col"), None),
    )
    return jax.shard_map(
        per_device,
        mesh=mesh,
        in_specs=placed,
        out_specs=(P(None, None, ("groups", "row"), "col"), P("groups", None, ("row", "col"))),
        check_vma=False,
    )
```

time: 663 us -> 231 us (0.35); the launches traced: 651 us -> 231 us
  other arithmetic: 279 us -> 9.58 us
  matrix products: 135 us -> 0.25 us
  blocking collectives: 0 us -> 57.6 us
  local copies, waits for them, and re-layouts: 59.8 us -> 12.4 us
  Pallas kernels: 0 us -> 40.3 us
  waiting for transfers between devices: 111 us -> 71.2 us
  loops' own time: 17.6 us -> 0 us
  between operations: 31.1 us -> 14.2 us
  starting transfers between devices: 18.1 us -> 25 us
    div x9 -> x0, other arithmetic: 200 us -> none  [the longest x5 102 us: lower_inverse(): rows_im.append(acc_im / low_re[row_idx, row_idx])]
    dot_general x138 -> x1, matrix products: 135 us -> 0.25 us  [gram_of(): full = jnp.einsum('ax,bx->ab', both, both, precision=highest_mode)]
    psum x1 -> x0, waiting for transfers between devices: 91.7 us -> none  [per_device(): total_grad = lax.psum(grad_cols, ('row', 'col'))]
    psum x0 -> x1, blocking collectives: none -> 57.6 us  [per_device(): gram = lax.psum(gram_of(own_probe, own_grad), ('row', 'col'))]
    reduce_scatter x0 -> x1, waiting for transfers between devices: none -> 48.6 us  [per_device(): lax.psum_scatter(grad_probe.reshape(modes, 2, pixels), ('row', 'col'), sc...]
    pallas_call x0 -> x2, Pallas kernels: none -> 40.3 us  [the longest x1 37.7 us: run_records(): pl.pallas_call(wave_kernel, out_shape=(jax.ShapeDtypeStruct(ext.shape, f3...]
    sub x8 -> x0, other arithmetic: 34.9 us -> none  [the longest x7 34.9 us: complex_cholesky(): numer_re = numer_re - (vec_re * pivot_re + vec_im * pivot_im)]
    select_n x7 -> x0, other arithmetic: 26.1 us -> none  [complex_cholesky(): cols_im.append(jnp.where(below, numer_im / diag_val, 0.0))]
  transfers between devices with their start and end apart: 9 -> 9, of which waited for: 3 -> 3; matrix products, arithmetic and copies ran while one was open for 46% -> 4% of each run, Pallas kernels for 0% -> 1%
where the time goes in v1:
time: 231 us
  waiting for transfers between devices  71.2 us (31%)
  blocking collectives  57.6 us (25%)
  Pallas kernels  40.3 us (17%)
  starting transfers between devices  25 us (11%)
  between operations  14.2 us (6%)
  local copies, waits for them, and re-layouts  12.4 us (5%)
  other arithmetic  9.58 us (4%)
    psum x1, blocking collectives, per_device(): gram = lax.psum(gram_of(own_probe, own_grad), ('row', 'col'))  57.6 us
    reduce_scatter x1, waiting for transfers between devices, per_device(): lax.psum_scatter(grad_probe.reshape(modes, 2, pixels), ('row', 'col'), sc...  48.6 us
    pallas_call x1, Pallas kernels, run_records(): pl.pallas_call(wave_kernel, out_shape=(jax.ShapeDtypeStruct(ext.shape, f3...  37.7 us
    ppermute x2, waiting for transfers between devices, with_halo(): before = lax.ppermute(last, axis, up)  22.6 us
    ppermute x2, starting transfers between devices, fold_axis(): lax.ppermute(lax.slice_in_dim(grad, half + inner, full, axis=dim), axis, up)  9.93 us
    ppermute x2, starting transfers between devices, with_halo(): before = lax.ppermute(last, axis, up)  9.86 us
    add x2, other arithmetic, fold_axis(): return core + jnp.concatenate([before, after], axis=dim)  4.66 us
  transfers between devices with their start and end apart: 9, of which 3 were waited for; matrix products, arithmetic and copies ran while one was open for 4% of the time, Pallas kernels for 1%

profile of v1, /device:TPU:0, one launch (start us, length us, event | category | flops | bytes accessed | tf_op | source)
XLA Modules:
  0.0 230.5 jit_solution(6999389617519137833)
XLA Ops:
  7.2 0.0 reduce-scatter.2.cloned.1.call-start
  7.2 1.4 fusion.13
  8.6 4.9 %collective-permute-start = (f32[4,2,64,256]{3,2,1,0:T(8,128)S(1)}, f32[4,2,64,256]{3,2,1,0:T(8,128)S(1)}, u32[]{:S(2)}, u32[]{:S(2)}) collective-permute-start(f32[4,2,64,256]{3,2,1,0:T(8,128)S(1)} %get-tuple-element.15), channel_id=1, source_target_pairs={{0,2},{2,4},{4,6},{6,8},{8,10},{10,12},{12,14},{1,3},{3,5},{5,7},{... | collective-permute-start | bytes 1572872 | tf_op jit(solution)/shard_map/ppermute | solution.py:257
  13.5 1.3 collective-permute-start.1
  14.8 21.1 %collective-permute-done = f32[4,2,64,256]{3,2,1,0:T(8,128)S(1)} collective-permute-done((f32[4,2,64,256]{3,2,1,0:T(8,128)S(1)}, f32[4,2,64,256]{3,2,1,0:T(8,128)S(1)}, u32[]{:S(2)}, u32[]{:S(2)}) %collective-permute-start) | collective-permute-done | bytes 524320 | tf_op jit(solution)/shard_map/ppermute | solution.py:257
  35.9 0.1 constant_dynamic-update-slice_fusion.1
  36.1 1.5 fusion.12
  37.6 1.3 collective-permute-start.3
  38.9 5.0 %collective-permute-start.2 = (f32[4,2,256,128]{3,2,1,0:T(8,128)}, f32[4,2,256,128]{3,2,1,0:T(8,128)}, u32[]{:S(2)}, u32[]{:S(2)}) collective-permute-start(f32[4,2,256,128]{3,2,1,0:T(8,128)} %get-tuple-element.12), channel_id=1, source_target_pairs={{0,1},{2,3},{4,5},{6,7},{8,9},{10,11},{12,13},{14,15},{16,17},{18,... | collective-permute-start | bytes 3145736 | tf_op jit(solution)/shard_map/ppermute | solution.py:257
  43.9 0.1 pad_add_fusion
  44.0 1.5 collective-permute-done.2
  45.5 4.0 %pad_maximum_fusion.ext = f32[4,2,256,512]{3,2,1,0:T(8,128)} fusion(f32[4,2,256,128]{3,2,1,0:T(8,128)} %collective-permute-done.3, f32[4,2,256,256]{3,2,1,0:T(8,128)S(1)} %constant_dynamic-update-slice_fusion, f32[4,2,256,128]{3,2,1,0:T(8,128)} %collective-permute-done.2), kind=kLoop, calls=%fused_computation | loop fusion | flops 2097152 | bytes 8388608 | tf_op jit(solution)/shard_map/concatenate | solution.py:259
  49.5 37.7 %records.1 = (f32[4,2,256,512]{3,2,1,0:T(8,128)}, f32[8,2,128,128]{3,2,1,0:T(8,128)S(1)}) custom-call(s32[2,2]{1,0:T(2,128)S(1)} %broadcast_subtract_fusion.places, f32[2,63]{1,0:T(2,128)S(1)} %copy-done.3, f32[4,2,256,512]{3,2,1,0:T(8,128)} %pad_maximum_fusion.ext, f32[8,2,128,128]{3,2,1,0:T(8,128)S(1)} %copy-done, f32[2,128,128]{2,1,0:T(8,128)S(1)} %copy-done.1, ...), custom_call_target="tpu_custom_call" | custom-call | tf_op jit(solution)/shard_map/records/pallas_call | solution.py:177
  87.2 3.1 %fusion.10 = (f32[4,2,256,128]{3,2,1,0:T(8,128)}, f32[4,2,256,128]{3,2,1,0:T(8,128)}) fusion(f32[4,2,256,512]{3,2,1,0:T(8,128)} %get-tuple-element.4), kind=kLoop, calls=%fused_computation.27 | loop fusion | bytes 4194304 | tf_op jit(solution)/shard_map/slice | solution.py:269
  90.3 1.3 collective-permute-start.5
  91.6 4.1 %collective-permute-start.4 = (f32[4,2,256,128]{3,2,1,0:T(8,128)}, f32[4,2,256,128]{3,2,1,0:T(8,128)}, u32[]{:S(2)}, u32[]{:S(2)}) collective-permute-start(f32[4,2,256,128]{3,2,1,0:T(8,128)} %get-tuple-element.8), channel_id=1, source_target_pairs={{0,1},{2,3},{4,5},{6,7},{8,9},{10,11},{12,13},{14,15},{16,17},{18,... | collective-permute-start | bytes 3145736 | tf_op jit(solution)/shard_map/ppermute | solution.py:269
  95.7 1.6 copy.13
  97.3 0.6 copy.14
  97.9 0.6 fusion.14.probe
  98.6 1.0 copy-done.5
  99.6 2.5 %maximum_add_fusion = f32[4,2,256,256]{3,2,1,0:T(8,128)S(1)} fusion(f32[4,2,256,128]{3,2,1,0:T(8,128)} %copy-done.5, f32[4,2,256,128]{3,2,1,0:T(8,128)} %collective-permute-done.4, f32[4,2,256,512]{3,2,1,0:T(8,128)} %get-tuple-element.4), kind=kLoop, calls=%fused_computation.1 | loop fusion | flops 1048576 | bytes 6291456 | tf_op jit(solution)/shard_map/add | solution.py:271
  102.1 0.9 fusion.11
  103.0 1.3 collective-permute-start.7
  104.2 5.8 %collective-permute-start.6 = (f32[4,2,64,256]{3,2,1,0:T(8,128)S(1)}, f32[4,2,64,256]{3,2,1,0:T(8,128)}, u32[]{:S(2)}, u32[]{:S(2)}) collective-permute-start(f32[4,2,64,256]{3,2,1,0:T(8,128)S(1)} %get-tuple-element.10), channel_id=1, source_target_pairs={{0,2},{2,4},{4,6},{6,8},{8,10},{10,12},{12,14},{1,3},{3,5},{5,7},{... | collective-permute-start | bytes 1572872 | tf_op jit(solution)/shard_map/ppermute | solution.py:269
  110.1 48.6 %reduce-scatter.2.cloned.1.call-done = f32[8,2,1024]{2,0,1:T(8,128)} async-done(((f32[8,2,16384]{2,0,1:T(8,128)}), f32[8,2,1024]{2,0,1:T(8,128)}) %reduce-scatter.2.cloned.1.call-update) | async-done | bytes 65552 | tf_op jit(solution)/shard_map/reduce_scatter | solution.py:288
  158.7 0.8 fusion.5
  159.5 0.2 fusion
  159.7 0.1 fusion.8
  159.8 57.6 %psum.7.gram = f32[2,16,16]{2,1,0:T(8,128)} all-reduce(f32[2,16,16]{2,1,0:T(8,128)S(1)} %pad_maximum_fusion.2), channel_id=1, replica_groups=mesh['groups'=2,'row'=8,'col'=2] {'row','col'}, use_global_device_ids=true, to_apply=%region_1.0 | all-reduce | flops 512 | bytes 4096 | tf_op jit(solution)/shard_map/psum | solution.py:292
  217.4 2.5 %solve.1 = f32[2,8,1024]{2,1,0:T(8,128)} custom-call(f32[2,16,16]{2,1,0:T(8,128)} %psum.7.gram, f32[2,8,1024]{2,1,0:T(8,128)} %fusion.14.probe, f32[2,8,1024]{2,1,0:T(8,128)} %bitcast.24), custom_call_target="tpu_custom_call" | custom-call | tf_op jit(solution)/shard_map/solve/pallas_call | solution.py:294
  220.0 1.5 copy.10
  221.5 2.2 slice_add_fusion
  (25 shorter events, 0.2 us)
Async XLA Ops:
  7.2 28.7 %copy-start.4 = (f32[4,2,128,256]{3,2,1,0:T(8,128)S(1)}, f32[4,2,128,256]{3,2,1,0:T(8,128)}, u32[]{:S(2)}) copy-start(f32[4,2,128,256]{3,2,1,0:T(8,128)} %param.6) | copy-start | bytes 3145732
  7.2 151.5 %reduce-scatter.2.cloned.1.call-start = ((), (), s32[]{:S(2)}) async-start(), calls=%async_computation.1 | async-start | bytes 1114112 | tf_op jit(solution)/shard_map/reduce_scatter | solution.py:288
  8.6 27.2 %collective-permute-start = (f32[4,2,64,256]{3,2,1,0:T(8,128)S(1)}, f32[4,2,64,256]{3,2,1,0:T(8,128)S(1)}, u32[]{:S(2)}, u32[]{:S(2)}) collective-permute-start(f32[4,2,64,256]{3,2,1,0:T(8,128)S(1)} %get-tuple-element.15), channel_id=1, source_target_pairs={{0,2},{2,4},{4,6},{6,8},{8,10},{10,12},{12,14},{1,3},{3,5},{5,7},{... | collective-permute-start | bytes 1572872 | tf_op jit(solution)/shard_map/ppermute | solution.py:257
  13.5 22.5 %collective-permute-start.1 = (f32[4,2,64,256]{3,2,1,0:T(8,128)S(1)}, f32[4,2,64,256]{3,2,1,0:T(8,128)S(1)}, u32[]{:S(2)}, u32[]{:S(2)}) collective-permute-start(f32[4,2,64,256]{3,2,1,0:T(8,128)S(1)} %get-tuple-element.14), channel_id=1, source_target_pairs={{2,0},{4,2},{6,4},{8,6},{10,8},{12,10},{14,12},{3,1},{5,3},{7,5},{... | collective-permute-start | bytes 1572872 | tf_op jit(solution)/shard_map/ppermute | solution.py:258
  36.0 7.9 %copy-start.6 = (s32[2,2]{1,0:T(2,128)S(1)}, s32[2,2]{1,0:T(2,128)}, u32[]{:S(2)}) copy-start(s32[2,2]{1,0:T(2,128)} %param.10) | copy-start | bytes 52
  37.6 6.4 %collective-permute-start.3 = (f32[4,2,256,128]{3,2,1,0:T(8,128)}, f32[4,2,256,128]{3,2,1,0:T(8,128)}, u32[]{:S(2)}, u32[]{:S(2)}) collective-permute-start(f32[4,2,256,128]{3,2,1,0:T(8,128)} %get-tuple-element.13), channel_id=1, source_target_pairs={{1,0},{3,2},{5,4},{7,6},{9,8},{11,10},{13,12},{15,14},{17,16},{19,... | collective-permute-start | bytes 3145736 | tf_op jit(solution)/shard_map/ppermute | solution.py:258
  38.9 6.6 %collective-permute-start.2 = (f32[4,2,256,128]{3,2,1,0:T(8,128)}, f32[4,2,256,128]{3,2,1,0:T(8,128)}, u32[]{:S(2)}, u32[]{:S(2)}) collective-permute-start(f32[4,2,256,128]{3,2,1,0:T(8,128)} %get-tuple-element.12), channel_id=1, source_target_pairs={{0,1},{2,3},{4,5},{6,7},{8,9},{10,11},{12,13},{14,15},{16,17},{18,... | collective-permute-start | bytes 3145736 | tf_op jit(solution)/shard_map/ppermute | solution.py:257
  44.0 5.5 %copy-start = (f32[8,2,128,128]{3,2,1,0:T(8,128)S(1)}, f32[8,2,128,128]{3,2,1,0:T(8,128)}, u32[]{:S(2)}) copy-start(f32[8,2,128,128]{3,2,1,0:T(8,128)} %probe.1) | copy-start | bytes 3145732
  44.0 5.5 %copy-start.1 = (f32[2,128,128]{2,1,0:T(8,128)S(1)}, f32[2,128,128]{2,1,0:T(8,128)}, u32[]{:S(2)}) copy-start(f32[2,128,128]{2,1,0:T(8,128)} %measured.1) | copy-start | bytes 393220
  44.0 5.5 %copy-start.2 = (f32[2,128,128]{2,1,0:T(8,128)S(1)}, f32[2,128,128]{2,1,0:T(8,128)}, u32[]{:S(2)}) copy-start(f32[2,128,128]{2,1,0:T(8,128)} %constant.27.clone.dft) | copy-start | bytes 393220
  44.0 5.5 %copy-start.3 = (f32[2,63]{1,0:T(2,128)S(1)}, f32[2,63]{1,0:T(2,128)}, u32[]{:S(2)}) copy-start(f32[2,63]{1,0:T(2,128)} %taps.1) | copy-start | bytes 1516
  90.3 8.3 %collective-permute-start.5 = (f32[4,2,256,128]{3,2,1,0:T(8,128)}, f32[4,2,256,128]{3,2,1,0:T(8,128)S(1)}, u32[]{:S(2)}, u32[]{:S(2)}) collective-permute-start(f32[4,2,256,128]{3,2,1,0:T(8,128)} %get-tuple-element.9), channel_id=1, source_target_pairs={{1,0},{3,2},{5,4},{7,6},{9,8},{11,10},{13,12},{15,14},{17,16},{19,... | collective-permute-start | bytes 3145736 | tf_op jit(solution)/shard_map/ppermute | solution.py:270
  91.6 8.0 %collective-permute-start.4 = (f32[4,2,256,128]{3,2,1,0:T(8,128)}, f32[4,2,256,128]{3,2,1,0:T(8,128)}, u32[]{:S(2)}, u32[]{:S(2)}) collective-permute-start(f32[4,2,256,128]{3,2,1,0:T(8,128)} %get-tuple-element.8), channel_id=1, source_target_pairs={{0,1},{2,3},{4,5},{6,7},{8,9},{10,11},{12,13},{14,15},{16,17},{18,... | collective-permute-start | bytes 3145736 | tf_op jit(solution)/shard_map/ppermute | solution.py:269
  98.6 1.0 copy-start.5
  103.0 118.5 %collective-permute-start.7 = (f32[4,2,64,256]{3,2,1,0:T(8,128)}, f32[4,2,64,256]{3,2,1,0:T(8,128)S(1)}, u32[]{:S(2)}, u32[]{:S(2)}) collective-permute-start(f32[4,2,64,256]{3,2,1,0:T(8,128)} %get-tuple-element.11), channel_id=1, source_target_pairs={{2,0},{4,2},{6,4},{8,6},{10,8},{12,10},{14,12},{3,1},{5,3},{7,5},{... | collective-permute-start | bytes 1572872 | tf_op jit(solution)/shard_map/ppermute | solution.py:270
  104.2 117.2 %collective-permute-start.6 = (f32[4,2,64,256]{3,2,1,0:T(8,128)S(1)}, f32[4,2,64,256]{3,2,1,0:T(8,128)}, u32[]{:S(2)}, u32[]{:S(2)}) collective-permute-start(f32[4,2,64,256]{3,2,1,0:T(8,128)S(1)} %get-tuple-element.10), channel_id=1, source_target_pairs={{0,2},{2,4},{4,6},{6,8},{8,10},{10,12},{12,14},{1,3},{3,5},{5,7},{... | collective-permute-start | bytes 1572872 | tf_op jit(solution)/shard_map/ppermute | solution.py:269
Sparse Core Ops, SparseCore 0:
  97.4 61.2 reduce-scatter.1

commit v2 on v1

--- a/solution.py
+++ b/solution.py
@@ -57,8 +57,8 @@
 
 
 def wave_kernel(
-    places, taps, ext, probe, measured, dft, gext, gprobe,
-    rights, lefts, waves, far, patch, gpatch, level,
+    places, taps, ext, probe, measured, dft, gext, chunks,
+    rights, lefts, waves, far, patch, gpatch, level, gprobe,
 ):
     modes, _, width, _ = probe.shape
     layers = ext.shape[0]
@@ -163,9 +163,14 @@
         return carry
 
     lax.fori_loop(0, records, one_record, 0)
-
-
-def run_records(places, taps, ext, probe, measured):
+    cores, chips, rows = chunks.shape[0], chunks.shape[1], chunks.shape[4]
+    for chip in range(chips):
+        for core in range(cores):
+            first = (chip * cores + core) * rows
+            chunks[core, chip] = gprobe[:, :, first : first + rows, :]
+
+
+def run_records(places, taps, ext, probe, measured, chunk_shape):
     modes, _, width, _ = probe.shape
     layers = ext.shape[0]
     idx = np.arange(width)
@@ -176,7 +181,7 @@
     f32 = jnp.float32
     return pl.pallas_call(
         wave_kernel,
-        out_shape=(jax.ShapeDtypeStruct(ext.shape, f32), jax.ShapeDtypeStruct(probe.shape, f32)),
+        out_shape=(jax.ShapeDtypeStruct(ext.shape, f32), jax.ShapeDtypeStruct(chunk_shape, f32)),
         in_specs=[smem, smem, vmem, vmem, vmem, vmem],
         out_specs=(vmem, vmem),
         scratch_shapes=[
@@ -187,6 +192,7 @@
             pltpu.VMEM((layers, 2, width, width), f32),
             pltpu.VMEM((layers, 2, width, width), f32),
             pltpu.VMEM((width, width), f32),
+            pltpu.VMEM(probe.shape, f32),
         ],
         compiler_params=pltpu.CompilerParams(vmem_limit_bytes=48 << 20),
         name="records",
@@ -231,44 +237,282 @@
     return data_re * scale_out, data_im * (-scale_out)
 
 
-def solve_kernel(scale_out, gram, probe, grad, out):
-    out_re, out_im = eliminate(gram[0], gram[1], probe[0], probe[1], grad[0], grad[1], scale_out)
+def remote(src, dst, send, recv, **device):
+    return pltpu.make_async_remote_copy(
+        src_ref=src, dst_ref=dst, send_sem=send, recv_sem=recv,
+        device_id=device, device_id_type=pl.DeviceIdType.MESH,
+    )
+
+
+def halo_kernel(rows, obj, ext, up_send, up_recv, down_send, down_recv, mid_send, mid_recv, top_send, top_recv, low_send, low_recv):
+    layers, _, tall, wide = obj.shape
+    half = EDGE // 2
+    row, col = lax.axis_index("row"), lax.axis_index("col")
+    mate = 1 - col
+    has_up, has_down = row + 1 < rows, row > 0
+    barrier = pltpu.get_barrier_semaphore()
+    pl.semaphore_signal(barrier, inc=1, device_id={"col": mate}, device_id_type=pl.DeviceIdType.MESH)
+
+    @pl.when(has_up)
+    def _():
+        pl.semaphore_signal(barrier, inc=1, device_id={"row": row + 1}, device_id_type=pl.DeviceIdType.MESH)
+
+    @pl.when(has_down)
+    def _():
+        pl.semaphore_signal(barrier, inc=1, device_id={"row": row - 1}, device_id_type=pl.DeviceIdType.MESH)
+
+    inner = jnp.logical_and(has_up, has_down)
+    pl.when(inner)(lambda: pl.semaphore_wait(barrier, 3))
+    pl.when(jnp.logical_not(inner))(lambda: pl.semaphore_wait(barrier, 2))
+
+    own = pl.ds(EDGE, wide)
+    top, mid, low = pl.ds(0, half), pl.ds(half, tall), pl.ds(half + tall, half)
+    mate_src = pl.ds(pl.multiple_of(mate * (wide - EDGE), EDGE), EDGE)
+    ext_src = pl.ds(pl.multiple_of(EDGE + mate * (wide - EDGE), EDGE), EDGE)
+    mate_dst = pl.ds(pl.multiple_of(col * (wide + EDGE), EDGE), EDGE)
+    blank = pl.ds(pl.multiple_of(col * (wide + EDGE), EDGE), EDGE)
+
+    def up(k):
+        return remote(obj.at[k, :, pl.ds(tall - half, half), :], ext.at[k, :, top, own], up_send.at[k], up_recv.at[k], row=row + 1)
+
+    def down(k):
+        return remote(obj.at[k, :, pl.ds(0, half), :], ext.at[k, :, low, own], down_send.at[k], down_recv.at[k], row=row - 1)
+
+    def across(k):
+        return remote(obj.at[k, :, :, mate_src], ext.at[k, :, mid, mate_dst], mid_send.at[k], mid_recv.at[k], col=mate)
+
+    def across_top(k):
+        return remote(ext.at[k, :, top, ext_src], ext.at[k, :, top, mate_dst], top_send.at[k], top_recv.at[k], col=mate)
+
+    def across_low(k):
+        return remote(ext.at[k, :, low, ext_src], ext.at[k, :, low, mate_dst], low_send.at[k], low_recv.at[k], col=mate)
+
+    for k in range(layers):
+        pl.when(has_up)(lambda k=k: up(k).start())
+        pl.when(has_down)(lambda k=k: down(k).start())
+    for k in range(layers):
+        across(k).start()
+    for k in range(layers):
+        ext[k, :, mid, own] = obj[k]
+        ext[k, :, :, blank] = jnp.zeros((2, tall + 2 * half, EDGE), jnp.float32)
+
+    @pl.when(jnp.logical_not(has_down))
+    def _():
+        ext[:, :, top, :] = jnp.zeros((layers, 2, half, wide + 2 * EDGE), jnp.float32)
+
+    @pl.when(jnp.logical_not(has_up))
+    def _():
+        ext[:, :, low, :] = jnp.zeros((layers, 2, half, wide + 2 * EDGE), jnp.float32)
+
+    def pass_top(k):
+        up(k).wait_recv()
+        across_top(k).start()
+
+    def pass_low(k):
+        down(k).wait_recv()
+        across_low(k).start()
+
+    for k in range(layers):
+        pl.when(has_down)(lambda k=k: pass_top(k))
+        pl.when(has_up)(lambda k=k: pass_low(k))
+    for k in range(layers):
+        across(k).wait()
+        pl.when(has_down)(lambda k=k: across_top(k).wait())
+        pl.when(has_up)(lambda k=k: across_low(k).wait())
+        pl.when(has_up)(lambda k=k: up(k).wait_send())
+        pl.when(has_down)(lambda k=k: down(k).wait_send())
+
+
+def run_halo(obj):
+    layers, parts, tall, wide = obj.shape
+    vmem = pl.BlockSpec(memory_space=pltpu.VMEM)
+    return pl.pallas_call(
+        functools.partial(halo_kernel, lax.axis_size("row")),
+        out_shape=jax.ShapeDtypeStruct((layers, parts, tall + EDGE, wide + 2 * EDGE), jnp.float32),
+        in_specs=[vmem],
+        out_specs=vmem,
+        scratch_shapes=[pltpu.SemaphoreType.DMA((layers,)) for _ in range(10)],
+        compiler_params=pltpu.CompilerParams(
+            collective_id=0, has_side_effects=True, vmem_limit_bytes=32 << 20
+        ),
+        name="halo",
+    )(obj)
+
+
+def tail_kernel(
+    rows, scale_out, gext, chunks, probe, folded, out,
+    from_mate, partial, parts, from_col, row_out, from_row, grams,
+    half_send, half_recv, col_send, col_recv, up_send, up_recv, down_send, down_recv,
+    part_send, part_recv, gram_send, gram_recv,
+):
+    layers, _, tall, wide = folded.shape
+    half = EDGE // 2
+    row, col = lax.axis_index("row"), lax.axis_index("col")
+    mate = 1 - col
+    has_up, has_down = row + 1 < rows, row > 0
+    devices = 2 * rows
+    me = row * 2 + col
+    barrier = pltpu.get_barrier_semaphore()
+
+    def greet(step, carry):
+        other = lax.rem(me + step, devices)
+        pl.semaphore_signal(
+            barrier, inc=1, device_id={"row": other // 2, "col": lax.rem(other, 2)},
+            device_id_type=pl.DeviceIdType.MESH,
+        )
+        return carry
+
+    lax.fori_loop(1, devices, greet, 0)
+    pl.semaphore_wait(barrier, devices - 1)
+
+    half_copy = remote(chunks.at[mate], from_mate, half_send, half_recv, col=mate)
+    half_copy.start()
+    mate_part = pl.ds(pl.multiple_of(mate * (wide + EDGE), EDGE), EDGE)
+    mate_part = pl.ds(pl.multiple_of((1 - col) * (wide + EDGE), EDGE), EDGE)
+
+    def across(k):
+        return remote(gext.at[k, :, :, mate_part], from_col.at[k], col_send.at[k], col_recv.at[k], col=mate)
+
+    for k in range(layers):
+        across(k).start()
+
+    def part_copy(other, slot):
+        return remote(partial.at[other], parts.at[slot], part_send.at[other], part_recv.at[slot], row=other)
+
+    half_copy.wait()
+    partial[...] = chunks[col] + from_mate[...]
+
+    def send_part(step, carry):
+        part_copy(lax.rem(row + step, rows), row).start()
+        return carry
+
+    lax.fori_loop(1, rows, send_part, 0)
+
+    def up(k):
+        return remote(row_out.at[k, 0], from_row.at[k, 0], up_send.at[k], up_recv.at[k], row=row + 1)
+
+    def down(k):
+        return remote(row_out.at[k, 1], from_row.at[k, 1], down_send.at[k], down_recv.at[k], row=row - 1)
+
+    for k in range(layers):
+        across(k).wait()
+        left = gext[k, :, :, pl.ds(EDGE, EDGE)]
+        right = gext[k, :, :, pl.ds(wide, EDGE)]
+        arrived = from_col[k]
+        left = jnp.where(col == 1, left + arrived, left)
+        right = jnp.where(col == 0, right + arrived, right)
+        both = jnp.concatenate([left, right], axis=2)
+        folded[k] = both[:, half : half + tall]
+        row_out[k, 0] = both[:, half + tall :]
+        row_out[k, 1] = both[:, :half]
+        pl.when(has_up)(lambda k=k: up(k).start())
+        pl.when(has_down)(lambda k=k: down(k).start())
+
+    def take_part(step, total):
+        slot = lax.rem(row + step, rows)
+        part_copy(slot, slot).wait_recv()
+        return total + parts[slot]
+
+    own = lax.fori_loop(1, rows, take_part, partial[row])
+    pixel_rows = own.shape[2]
+    parts[row] = own
+
+    def columns(part):
+        return jnp.concatenate([parts[row, :, part, r, :] for r in range(pixel_rows)], axis=1)
+
+    grad_re, grad_im = columns(0), columns(1)
+    probe_re, probe_im = probe[0], probe[1]
+    stack = jnp.concatenate([probe_re, grad_re, probe_im, grad_im], axis=0)
+    padded = jnp.concatenate([stack, stack, stack, stack], axis=0)
+    grams[me] = lax.dot_general(
+        stack, padded, (((1,), (1,)), ((), ())), precision=highest_mode, preferred_element_type=jnp.float32
+    )
+
+    def gram_copy(other, slot):
+        return remote(
+            grams.at[me], grams.at[slot], gram_send.at[other], gram_recv.at[slot],
+            row=other // 2, col=lax.rem(other, 2),
+        )
+
+    def send_gram(step, carry):
+        gram_copy(lax.rem(me + step, devices), me).start()
+        return carry
+
+    lax.fori_loop(1, devices, send_gram, 0)
+
+    def wait_gram(step, carry):
+        other = lax.rem(me + step, devices)
+        gram_copy(other, other).wait_recv()
+        return carry
+
+    lax.fori_loop(1, devices, wait_gram, 0)
+    total = lax.fori_loop(1, devices, lambda slot, acc: acc + grams[slot], grams[0])
+    count = stack.shape[0] // 2
+    gram_re = total[:count, :count] + total[count:, count : 2 * count]
+    gram_im = total[:count, count : 2 * count] - total[count:, :count]
+    out_re, out_im = eliminate(gram_re, gram_im, probe_re, probe_im, grad_re, grad_im, scale_out)
     out[0] = out_re
     out[1] = out_im
 
-
-def gram_of(first, second):
-    stacked = jnp.concatenate([first, second], axis=0)
-    both = jnp.concatenate([stacked[:, 0], stacked[:, 1]], axis=0)
-    full = jnp.einsum("ax,bx->ab", both, both, precision=highest_mode)
-    count = stacked.shape[0]
-    return jnp.stack(
-        [full[:count, :count] + full[count:, count:], full[:count, count:] - full[count:, :count]]
-    )
-
-
-def with_halo(array, sides):
-    for axis, dim, width in sides:
-        devices, length = (lax.axis_size(axis), array.shape[dim])
-        up = [(i, i + 1) for i in range(devices - 1)]
-        down = [(j, i) for i, j in up]
-        last = lax.slice_in_dim(array, length - width, length, axis=dim)
-        first = lax.slice_in_dim(array, 0, width, axis=dim)
-        before = lax.ppermute(last, axis, up)
-        after = lax.ppermute(first, axis, down)
-        array = jnp.concatenate([before, array, after], axis=dim)
-    return array
-
-
-def fold_axis(grad, axis, dim, half):
-    devices, full = lax.axis_size(axis), grad.shape[dim]
-    inner = full - 2 * half
-    up = [(i, i + 1) for i in range(devices - 1)]
-    down = [(j, i) for i, j in up]
-    core = lax.slice_in_dim(grad, half, half + inner, axis=dim)
-    before = lax.ppermute(lax.slice_in_dim(grad, half + inner, full, axis=dim), axis, up)
-    after = lax.ppermute(lax.slice_in_dim(grad, 0, half, axis=dim), axis, down)
-    return core + jnp.concatenate([before, after], axis=dim)
+    def take_top(k):
+        up(k).wait_recv()
+        folded[k, :, :half] = folded[k, :, :half] + from_row[k, 0]
+
+    def take_low(k):
+        down(k).wait_recv()
+        folded[k, :, tall - half :] = folded[k, :, tall - half :] + from_row[k, 1]
+
+    for k in range(layers):
+        pl.when(has_down)(lambda k=k: take_top(k))
+        pl.when(has_up)(lambda k=k: take_low(k))
+    for k in range(layers):
+        pl.when(has_up)(lambda k=k: up(k).wait_send())
+        pl.when(has_down)(lambda k=k: down(k).wait_send())
+
+    def finish(step, carry):
+        part_copy(lax.rem(row + step, rows), row).wait_send()
+        return carry
+
+    lax.fori_loop(1, rows, finish, 0)
+
+    def finish_gram(step, carry):
+        gram_copy(lax.rem(me + step, devices), me).wait_send()
+        return carry
+
+    lax.fori_loop(1, devices, finish_gram, 0)
+
+
+def run_tail(gext, chunks, probe, tile_shape, scale_out):
+    layers, parts, tall, wide = tile_shape
+    _, rows, modes, _, pixel_rows, lanes = chunks.shape
+    half = EDGE // 2
+    f32 = jnp.float32
+    vmem = pl.BlockSpec(memory_space=pltpu.VMEM)
+    sems = pltpu.SemaphoreType.DMA
+    return pl.pallas_call(
+        functools.partial(tail_kernel, rows, scale_out),
+        out_shape=(
+            jax.ShapeDtypeStruct(tile_shape, f32),
+            jax.ShapeDtypeStruct((2, modes, pixel_rows * lanes), f32),
+        ),
+        in_specs=[vmem] * 3,
+        out_specs=(vmem, vmem),
+        scratch_shapes=[
+            pltpu.VMEM(chunks.shape[1:], f32),
+            pltpu.VMEM(chunks.shape[1:], f32),
+            pltpu.VMEM(chunks.shape[1:], f32),
+            pltpu.VMEM((layers, parts, tall + EDGE, EDGE), f32),
+            pltpu.VMEM((layers, 2, parts, half, wide), f32),
+            pltpu.VMEM((layers, 2, parts, half, wide), f32),
+            pltpu.VMEM((2 * rows, 4 * modes, 128), f32),
+            sems, sems, sems((layers,)), sems((layers,)), sems((layers,)), sems((layers,)), sems((layers,)), sems((layers,)),
+            sems((rows,)), sems((rows,)), sems((2 * rows,)), sems((2 * rows,)),
+        ],
+        compiler_params=pltpu.CompilerParams(
+            collective_id=1, has_side_effects=True, vmem_limit_bytes=48 << 20
+        ),
+        name="tail",
+    )(gext, chunks, probe)
 
 
 def per_device(object_slices, probe, taps, measured, positions):
@@ -276,26 +520,19 @@
     half = width // 2
     tile_rows = object_slices.shape[2]
     tile_cols = object_slices.shape[3]
-    ext = with_halo(object_slices, (("row", 2, half), ("col", 3, EDGE)))
+    rows = lax.axis_size("row")
+    ext = run_halo(object_slices)
     anchor = jnp.stack(
         [lax.axis_index("row") * tile_rows - half, lax.axis_index("col") * tile_cols - EDGE]
     )
     places = positions - anchor[None, :]
-    grad_ext, grad_probe = run_records(places, taps, ext, probe, measured)
-    pixels = width * width
-    share = pixels // (lax.axis_size("row") * lax.axis_size("col"))
-    start = lax.axis_index(("row", "col")) * share
-    own_grad = lax.psum_scatter(
-        grad_probe.reshape(modes, 2, pixels), ("row", "col"), scatter_dimension=2, tiled=True
-    )
-    own_probe = lax.dynamic_slice_in_dim(probe.reshape(modes, 2, pixels), start, share, 2)
-    gram = lax.psum(gram_of(own_probe, own_grad), ("row", "col"))
-    folded = fold_axis(fold_axis(grad_ext, "col", 3, EDGE), "row", 2, half)
-    new_probe = pl.pallas_call(
-        functools.partial(solve_kernel, float(width)),
-        out_shape=jax.ShapeDtypeStruct((2, modes, share), jnp.float32),
-        name="solve",
-    )(gram, own_probe.transpose(1, 0, 2), own_grad.transpose(1, 0, 2))
+    pixel_rows = width // (2 * rows)
+    chunk_shape = (2, rows, modes, 2, pixel_rows, width)
+    grad_ext, chunks = run_records(places, taps, ext, probe, measured, chunk_shape)
+    share = pixel_rows * width
+    own_probe = lax.dynamic_slice_in_dim(probe, lax.axis_index(("row", "col")) * pixel_rows, pixel_rows, 2)
+    own_probe = own_probe.reshape(modes, 2, share).transpose(1, 0, 2)
+    folded, new_probe = run_tail(grad_ext, chunks, own_probe, object_slices.shape, float(width))
     return (folded, new_probe.transpose(1, 0, 2))
 
 

time: 231 us -> 114 us (0.49)
  the two profiles are of different devices: /device:TPU:0 before, /device:TPU:13 now
where the time goes in v2:
time: 114 us
  Pallas kernels  108 us (95%)
  local copies, waits for them, and re-layouts  4.86 us (4%)
    pallas_call x1, Pallas kernels, run_tail(): pl.pallas_call(functools.partial(tail_kernel, rows, scale_out), out_shape...  42.3 us
    pallas_call x1, Pallas kernels, run_records(): pl.pallas_call(wave_kernel, out_shape=(jax.ShapeDtypeStruct(ext.shape, f3...  37.7 us
    pallas_call x1, Pallas kernels, run_halo(): pl.pallas_call(functools.partial(halo_kernel, lax.axis_size('row')), out_...  27.6 us
    unnamed x14, local copies, waits for them, and re-layouts  4.82 us

profile of v2, /device:TPU:13, one launch (start us, length us, event | category | flops | bytes accessed | tf_op | source)
XLA Modules:
  0.0 114.0 jit_solution(83613179829301742)
XLA Ops:
  0.6 0.0 copy-start.1
  0.6 0.1 pad_add_fusion
  0.7 0.8 broadcast_subtract_fusion.places
  1.5 0.0 copy-start.2
  1.5 1.2 %copy-done.2 = f32[4,2,128,256]{3,2,1,0:T(8,128)S(1)} copy-done((f32[4,2,128,256]{3,2,1,0:T(8,128)S(1)}, f32[4,2,128,256]{3,2,1,0:T(8,128)}, u32[]{:S(2)}) %copy-start.2) | copy-done | bytes 1048600
  2.7 0.0 copy-start.3
  2.7 0.0 copy-start.4
  2.7 0.0 copy-start.5
  2.7 27.6 %halo.1.ext = f32[4,2,256,512]{3,2,1,0:T(8,128)S(1)} custom-call(f32[4,2,128,256]{3,2,1,0:T(8,128)S(1)} %copy-done.2), custom_call_target="tpu_custom_call" | custom-call | tf_op jit(solution)/shard_map/halo/pallas_call | solution.py:329
  30.3 0.0 copy-start
  30.3 1.9 %copy-done = f32[4,2,256,512]{3,2,1,0:T(8,128)} copy-done((f32[4,2,256,512]{3,2,1,0:T(8,128)}, f32[4,2,256,512]{3,2,1,0:T(8,128)S(1)}, u32[]{:S(2)}) %copy-start) | copy-done | bytes 4194328
  32.2 0.0 copy-done.1
  32.2 0.0 copy-done.3
  32.2 0.0 copy-done.4
  32.2 0.0 copy-done.5
  32.2 37.7 %records.1 = (f32[4,2,256,512]{3,2,1,0:T(8,128)}, f32[2,8,8,2,8,128]{5,4,3,2,1,0:T(8,128)S(1)}) custom-call(s32[2,2]{1,0:T(2,128)S(1)} %broadcast_subtract_fusion.places, f32[2,63]{1,0:T(2,128)S(1)} %copy-done.5, f32[4,2,256,512]{3,2,1,0:T(8,128)} %copy-done, f32[8,2,128,128]{3,2,1,0:T(8,128)S(1)} %copy-done.1, f32[2,128,128]{2,1,0:T(8,128)S(1)} %copy-done.3, ...), custom_call_target="tpu_custom_call" | custom-call | tf_op jit(solution)/shard_map/records/pallas_call | solution.py:182
  70.0 42.3 %tail.1 = (f32[4,2,128,256]{3,2,1,0:T(8,128)S(1)}, f32[2,8,1024]{2,1,0:T(8,128)S(1)}) custom-call(f32[4,2,256,512]{3,2,1,0:T(8,128)} %get-tuple-element.6.gext, f32[2,8,8,2,8,128]{5,4,3,2,1,0:T(8,128)S(1)} %get-tuple-element.7.chunks, f32[2,8,1024]{2,1,0:T(8,128)S(1)} %bitcast.8), custom_call_target="tpu_custom_call" | custom-call | tf_op jit(solution)/shard_map/tail/pallas_call | solution.py:492
  112.4 0.7 copy.9
  113.1 1.0 copy.13
  (2 shorter events, 0.0 us)
Async XLA Ops:
  0.6 31.6 %copy-start.1 = (f32[8,2,128,128]{3,2,1,0:T(8,128)S(1)}, f32[8,2,128,128]{3,2,1,0:T(8,128)}, u32[]{:S(2)}) copy-start(f32[8,2,128,128]{3,2,1,0:T(8,128)} %probe.1) | copy-start | bytes 3145732
  1.5 1.2 %copy-start.2 = (f32[4,2,128,256]{3,2,1,0:T(8,128)S(1)}, f32[4,2,128,256]{3,2,1,0:T(8,128)}, u32[]{:S(2)}) copy-start(f32[4,2,128,256]{3,2,1,0:T(8,128)} %obj.1) | copy-start | bytes 3145732
  2.7 29.5 %copy-start.3 = (f32[2,128,128]{2,1,0:T(8,128)S(1)}, f32[2,128,128]{2,1,0:T(8,128)}, u32[]{:S(2)}) copy-start(f32[2,128,128]{2,1,0:T(8,128)} %measured.1) | copy-start | bytes 393220
  2.7 29.5 %copy-start.4 = (f32[2,128,128]{2,1,0:T(8,128)S(1)}, f32[2,128,128]{2,1,0:T(8,128)}, u32[]{:S(2)}) copy-start(f32[2,128,128]{2,1,0:T(8,128)} %constant.25.clone.dft) | copy-start | bytes 393220
  2.7 29.5 %copy-start.5 = (f32[2,63]{1,0:T(2,128)S(1)}, f32[2,63]{1,0:T(2,128)}, u32[]{:S(2)}) copy-start(f32[2,63]{1,0:T(2,128)} %taps.1) | copy-start | bytes 1516
  30.3 1.9 %copy-start = (f32[4,2,256,512]{3,2,1,0:T(8,128)}, f32[4,2,256,512]{3,2,1,0:T(8,128)S(1)}, u32[]{:S(2)}) copy-start(f32[4,2,256,512]{3,2,1,0:T(8,128)S(1)} %halo.1.ext) | copy-start | bytes 12582916

commit v3 on v1

v3 whole, which is shorter than its diff:
```python
import functools
import math

import jax
import jax.numpy as jnp
import numpy as np
from jax import lax
from jax.experimental import pallas as pl
from jax.experimental.pallas import tpu as pltpu
from jax.sharding import PartitionSpec as P

highest_mode = lax.Precision.HIGHEST
EDGE = 128


def split(value):
    high = value.astype(jnp.bfloat16)
    low = (value - high.astype(jnp.float32)).astype(jnp.bfloat16)
    return high, low


def block_matrix(mat_re, mat_im):
    top = jnp.concatenate([mat_re, -mat_im], axis=1)
    bottom = jnp.concatenate([mat_im, mat_re], axis=1)
    return jnp.concatenate([top, bottom], axis=0)


def store_matrices(mat_re, mat_im, trans_re, trans_im, slot, rights, lefts):
    plain = split(block_matrix(mat_re, mat_im))
    turned = split(block_matrix(trans_re, -trans_im))
    for place, (right, left) in ((slot, (turned, plain)), (slot + 2, (plain, turned))):
        rights[place] = jnp.concatenate([right[0], right[0], right[1]], axis=0)
        lefts[place] = jnp.concatenate([left[0], left[0], left[1]], axis=1)


def both_sides(waves, right, left):
    width = waves[0][0].shape[0]
    rows = jnp.concatenate([jnp.concatenate([re, im], axis=1) for re, im in waves], axis=0)
    high, low = split(rows)
    mid = jnp.dot(
        jnp.concatenate([high, low, high], axis=1), right, preferred_element_type=jnp.float32
    )
    parts = []
    for idx in range(len(waves)):
        part = mid[idx * width : (idx + 1) * width]
        parts.append(jnp.concatenate([part[:, :width], part[:, width:]], axis=0))
    cols = jnp.concatenate(parts, axis=1)
    high, low = split(cols)
    out = jnp.dot(
        left, jnp.concatenate([high, low, high], axis=0), preferred_element_type=jnp.float32
    )
    result = []
    for idx in range(len(waves)):
        part = out[:, idx * width : (idx + 1) * width]
        result.append((part[:width], part[width:]))
    return result


def eliminate(gram_re, gram_im, probe_re, probe_im, grad_re, grad_im, scale_out):
    modes = probe_re.shape[0]
    idx = lax.broadcasted_iota(jnp.int32, (modes, modes), 0)
    lane = lax.broadcasted_iota(jnp.int32, (modes, modes), 1)
    diag = idx == lane
    w_pp, w_gg = gram_re[:modes, :modes], gram_re[modes:, modes:]
    trace_pp = jnp.sum(jnp.where(diag, w_pp, 0.0), keepdims=True)
    trace_gg = jnp.sum(jnp.where(diag, w_gg, 0.0), keepdims=True)
    factor = 0.5 * jnp.sqrt(trace_pp / (trace_gg + 1e-06))
    new_re = w_pp - factor * (gram_re[:modes, modes:] + gram_re[modes:, :modes]) + factor * factor * w_gg
    new_im = (
        gram_im[:modes, :modes]
        - factor * (gram_im[:modes, modes:] + gram_im[modes:, :modes])
        + factor * factor * gram_im[modes:, modes:]
    )
    data_re = probe_re - factor * grad_re
    data_im = factor * grad_im - probe_im
    below = lax.broadcasted_iota(jnp.int32, (modes, 1), 0)
    for step in range(modes):
        pivot = new_re[step : step + 1, step : step + 1]
        scale = 1.0 / jnp.sqrt(pivot)
        keep = below > step
        coef_re = jnp.where(keep, new_re[:, step : step + 1] * scale, 0.0)
        coef_im = jnp.where(keep, new_im[:, step : step + 1] * scale, 0.0)
        at = below == step

        def update(re, im):
            row_re = re[step : step + 1] * scale
            row_im = im[step : step + 1] * scale
            next_re = re - (coef_re * row_re - coef_im * row_im)
            next_im = im - (coef_re * row_im + coef_im * row_re)
            return jnp.where(at, row_re, next_re), jnp.where(at, row_im, next_im)

        data_re, data_im = update(data_re, data_im)
        new_re, new_im = update(new_re, new_im)
    return data_re * scale_out, data_im * (-scale_out)


def remote(src, dst, send, recv, **device):
    return pltpu.make_async_remote_copy(
        src_ref=src, dst_ref=dst, send_sem=send, recv_sem=recv,
        device_id=device, device_id_type=pl.DeviceIdType.MESH,
    )


def make_matrices(taps, dft, width, rights, lefts):
    count = taps.shape[1]
    reach = count // 2
    shape = (width, width)
    offset = lax.broadcasted_iota(jnp.int32, shape, 1) - lax.broadcasted_iota(jnp.int32, shape, 0)
    bands = [jnp.zeros(shape, jnp.float32) for _ in range(4)]
    for idx in range(count):
        ahead = offset == idx - reach
        behind = offset == reach - idx
        bands[0] = jnp.where(ahead, taps[0, idx], bands[0])
        bands[1] = jnp.where(ahead, taps[1, idx], bands[1])
        bands[2] = jnp.where(behind, taps[0, idx], bands[2])
        bands[3] = jnp.where(behind, taps[1, idx], bands[3])
    store_matrices(*bands, 0, rights, lefts)
    store_matrices(dft[0], dft[1], dft[0], dft[1], 1, rights, lefts)


def fused_kernel(
    rows, scale_out, group,
    places, taps, obj, probe, own_probe, measured, dft, folded, out,
    ext0, ext1, ext2, ext3, rights, lefts, waves, far, patch, gpatch, level, gprobe, gext,
    chunks, from_mate, partial, parts, from_col, row_out, from_row, grams,
    pick_rows, pick_cols, put_rows, put_cols,
    hup_send, hup_recv, hdown_send, hdown_recv, mid_send, mid_recv, top_send, top_recv, low_send, low_recv,
    half_send, half_recv, col_send, col_recv, up_send, up_recv, down_send, down_recv,
    part_send, part_recv, gram_send, gram_recv,
):
    exts = (ext0, ext1, ext2, ext3)
    layers, _, tall, wide = obj.shape
    modes, _, width, _ = probe.shape
    records = measured.shape[0]
    half = EDGE // 2
    row, col = lax.axis_index("row"), lax.axis_index("col")
    mate = 1 - col
    has_up, has_down = row + 1 < rows, row > 0
    devices = 2 * rows
    me = row * 2 + col
    weight = 1.0 / (8.0 * modes)
    barrier = pltpu.get_barrier_semaphore()

    def greet(step, carry):
        other = lax.rem(me + step, devices)
        pl.semaphore_signal(
            barrier, inc=1, device_id={"row": other // 2, "col": lax.rem(other, 2)},
            device_id_type=pl.DeviceIdType.MESH,
        )
        return carry

    lax.fori_loop(1, devices, greet, 0)
    pl.semaphore_wait(barrier, devices - 1)

    own = pl.ds(EDGE, wide)
    top, mid, low = pl.ds(0, half), pl.ds(half, tall), pl.ds(half + tall, half)
    mate_src = pl.ds(pl.multiple_of(mate * (wide - EDGE), EDGE), EDGE)
    ext_src = pl.ds(pl.multiple_of(EDGE + mate * (wide - EDGE), EDGE), EDGE)
    mate_dst = pl.ds(pl.multiple_of(col * (wide + EDGE), EDGE), EDGE)

    def halo_up(k):
        return remote(obj.at[k, :, pl.ds(tall - half, half), :], exts[k].at[:, top, own], hup_send.at[k], hup_recv.at[k], row=row + 1)

    def halo_down(k):
        return remote(obj.at[k, :, pl.ds(0, half), :], exts[k].at[:, low, own], hdown_send.at[k], hdown_recv.at[k], row=row - 1)

    def halo_mid(k):
        return remote(obj.at[k, :, :, mate_src], exts[k].at[:, mid, mate_dst], mid_send.at[k], mid_recv.at[k], col=mate)

    def halo_top(k):
        return remote(exts[k].at[:, top, ext_src], exts[k].at[:, top, mate_dst], top_send.at[k], top_recv.at[k], col=mate)

    def halo_low(k):
        return remote(exts[k].at[:, low, ext_src], exts[k].at[:, low, mate_dst], low_send.at[k], low_recv.at[k], col=mate)

    for k in range(layers):
        pl.when(has_up)(lambda k=k: halo_up(k).start())
        pl.when(has_down)(lambda k=k: halo_down(k).start())
        halo_mid(k).start()
    for k in range(layers):
        exts[k][:, mid, own] = obj[k]
        exts[k][:, :, mate_dst] = jnp.zeros((2, tall + 2 * half, EDGE), jnp.float32)

    @pl.when(jnp.logical_not(has_down))
    def _():
        for k in range(layers):
            exts[k][:, top, :] = jnp.zeros((2, half, wide + 2 * EDGE), jnp.float32)

    @pl.when(jnp.logical_not(has_up))
    def _():
        for k in range(layers):
            exts[k][:, low, :] = jnp.zeros((2, half, wide + 2 * EDGE), jnp.float32)

    def pass_top(k):
        halo_up(k).wait_recv()
        halo_top(k).start()

    def pass_low(k):
        halo_down(k).wait_recv()
        halo_low(k).start()

    def pass_halo(k):
        pl.when(has_down)(lambda: pass_top(k))
        pl.when(has_up)(lambda: pass_low(k))

    def end_halo(k):
        halo_mid(k).wait()
        pl.when(has_down)(lambda: halo_top(k).wait())
        pl.when(has_up)(lambda: halo_low(k).wait())
        pl.when(has_up)(lambda: halo_up(k).wait_send())
        pl.when(has_down)(lambda: halo_down(k).wait_send())

    make_matrices(taps, dft, width, rights, lefts)
    level[...] = jnp.zeros_like(level)
    pass_halo(0)

    def one_hot(shape, dim, shift):
        first = lax.broadcasted_iota(jnp.int32, shape, dim)
        second = lax.broadcasted_iota(jnp.int32, shape, 1 - dim)
        return jnp.where(first == second + shift, 1.0, 0.0).astype(jnp.bfloat16)

    full_rows, full_cols = tall + 2 * half, wide + 2 * EDGE
    for rec in range(records):
        r, c = places[rec, 0], places[rec, 1]
        pick = one_hot((width, full_rows), 1, r)
        pick_rows[rec] = jnp.concatenate([pick, pick], axis=1)
        pick = one_hot((2 * EDGE, width), 0, lax.rem(c, EDGE))
        pick_cols[rec] = jnp.concatenate([pick, pick], axis=0)
        put = one_hot((full_rows, width), 0, r)
        put_rows[rec] = jnp.concatenate([put, put], axis=1)
        put = one_hot((width, full_cols), 1, c)
        put_cols[pl.ds(rec * 2 * width, 2 * width)] = jnp.concatenate([put, put], axis=0)

    for layer in range(layers):
        end_halo(layer)
        for rec in range(records):
            start = jnp.zeros((1, 2 * EDGE), jnp.int32) + places[rec, 1]
            pieces = []
            for part in range(2):
                image = exts[layer][part]
                piece = image[:, 2 * EDGE : 4 * EDGE]
                piece = jnp.where(start < 2 * EDGE, image[:, EDGE : 3 * EDGE], piece)
                pieces.append(jnp.where(start < EDGE, image[:, : 2 * EDGE], piece))
            piece = jnp.concatenate(split(jnp.concatenate(pieces, axis=0)), axis=1)
            piece = jnp.dot(piece, pick_cols[rec], preferred_element_type=jnp.float32)
            piece = jnp.concatenate([piece[:full_rows], piece[full_rows:]], axis=1)
            piece = jnp.concatenate(split(piece), axis=0)
            piece = jnp.dot(pick_rows[rec], piece, preferred_element_type=jnp.float32)
            patch[rec, layer, 0] = piece[:, :width]
            patch[rec, layer, 1] = piece[:, width:]
        if layer + 1 < layers:
            pass_halo(layer + 1)

        def forward(step, carry, layer=layer):
            base = step * group
            now = []
            for rec in range(records):
                obj_re, obj_im = patch[rec, layer, 0], patch[rec, layer, 1]
                for k in range(group):
                    if layer:
                        a, b = waves[rec, layer - 1, base + k, 0], waves[rec, layer - 1, base + k, 1]
                    else:
                        a, b = probe[base + k, 0], probe[base + k, 1]
                    now.append((a * obj_re - b * obj_im, a * obj_im + b * obj_re))
            slot = 0 if layer + 1 < layers else 1
            now = both_sides(now, rights[slot], lefts[slot])
            for rec in range(records):
                total = None
                for k in range(group):
                    a, b = now[rec * group + k]
                    if layer + 1 < layers:
                        waves[rec, layer, base + k, 0] = a
                        waves[rec, layer, base + k, 1] = b
                    else:
                        far[rec, base + k, 0] = a
                        far[rec, base + k, 1] = b
                        power = a * a + b * b
                        total = power if total is None else total + power
                if total is not None:
                    level[rec] = level[rec] + total
            return carry

        lax.fori_loop(0, modes // group, forward, 0)

    level[...] = (2.0 * weight) * (level[...] - measured[...])
    gpatch[...] = jnp.zeros_like(gpatch)

    mate_part = pl.ds(pl.multiple_of(mate * (wide + EDGE), EDGE), EDGE)

    def across(k):
        return remote(gext.at[k, :, :, mate_part], from_col.at[k], col_send.at[k], col_recv.at[k], col=mate)

    def up(k):
        return remote(row_out.at[k, 0], from_row.at[k, 0], up_send.at[k], up_recv.at[k], row=row + 1)

    def down(k):
        return remote(row_out.at[k, 1], from_row.at[k, 1], down_send.at[k], down_recv.at[k], row=row - 1)

    def scatter(k):
        pieces = []
        for rec in range(records):
            piece = jnp.concatenate([gpatch[rec, k, 0], gpatch[rec, k, 1]], axis=1)
            piece = jnp.concatenate(split(piece), axis=0)
            piece = jnp.dot(put_rows[rec], piece, preferred_element_type=jnp.float32)
            pieces += split(jnp.concatenate([piece[:, :width], piece[:, width:]], axis=0))
        image = jnp.dot(jnp.concatenate(pieces, axis=1), put_cols[...], preferred_element_type=jnp.float32)
        gext[k, 0] = image[:full_rows]
        gext[k, 1] = image[full_rows:]

    def send_rows(k):
        across(k).wait()
        left = gext[k, :, :, pl.ds(EDGE, EDGE)]
        right = gext[k, :, :, pl.ds(wide, EDGE)]
        arrived = from_col[k]
        left = jnp.where(col == 1, left + arrived, left)
        right = jnp.where(col == 0, right + arrived, right)
        both = jnp.concatenate([left, right], axis=2)
        folded[k] = both[:, half : half + tall]
        row_out[k, 0] = both[:, half + tall :]
        row_out[k, 1] = both[:, :half]
        pl.when(has_up)(lambda: up(k).start())
        pl.when(has_down)(lambda: down(k).start())

    for layer in reversed(range(layers)):

        def backward(step, carry, layer=layer):
            base = step * group
            now = []
            for rec in range(records):
                for k in range(group):
                    a, b = far[rec, base + k, 0], far[rec, base + k, 1]
                    if layer + 1 == layers:
                        a, b = a * level[rec], b * level[rec]
                    now.append((a, b))
            slot = 2 if layer + 1 < layers else 3
            now = both_sides(now, rights[slot], lefts[slot])
            sums = [[None, None] for _ in range(group)]
            for rec in range(records):
                sum_re, sum_im = gpatch[rec, layer, 0], gpatch[rec, layer, 1]
                obj_re, obj_im = patch[rec, layer, 0], patch[rec, layer, 1]
                for k in range(group):
                    a, b = now[rec * group + k]
                    if layer:
                        c, d = waves[rec, layer - 1, base + k, 0], waves[rec, layer - 1, base + k, 1]
                    else:
                        c, d = probe[base + k, 0], probe[base + k, 1]
                    sum_re = sum_re + (a * c + b * d)
                    sum_im = sum_im + (b * c - a * d)
                    e, f = a * obj_re + b * obj_im, b * obj_re - a * obj_im
                    if layer:
                        far[rec, base + k, 0] = e
                        far[rec, base + k, 1] = f
                    elif rec:
                        sums[k] = [sums[k][0] + e, sums[k][1] + f]
                    else:
                        sums[k] = [e, f]
                gpatch[rec, layer, 0] = sum_re
                gpatch[rec, layer, 1] = sum_im
            if not layer:
                for k in range(group):
                    gprobe[base + k, 0] = sums[k][0]
                    gprobe[base + k, 1] = sums[k][1]
            return carry

        lax.fori_loop(0, modes // group, backward, 0)
        if layer:
            scatter(layer)
            across(layer).start()
            if layer + 1 < layers:
                send_rows(layer + 1)

    pixel_rows = chunks.shape[4]
    for chip in range(rows):
        for core in range(2):
            first = (chip * 2 + core) * pixel_rows
            chunks[core, chip] = gprobe[:, :, first : first + pixel_rows, :]
    half_copy = remote(chunks.at[mate], from_mate, half_send, half_recv, col=mate)
    half_copy.start()
    scatter(0)
    across(0).start()

    def part_copy(other, slot):
        return remote(partial.at[other], parts.at[slot], part_send.at[other], part_recv.at[slot], row=other)

    half_copy.wait()
    partial[...] = chunks[col] + from_mate[...]

    def send_part(step, carry):
        part_copy(lax.rem(row + step, rows), row).start()
        return carry

    lax.fori_loop(1, rows, send_part, 0)
    send_rows(1)
    send_rows(0)

    def take_part(step, total):
        slot = lax.rem(row + step, rows)
        part_copy(slot, slot).wait_recv()
        return total + parts[slot]

    parts[row] = lax.fori_loop(1, rows, take_part, partial[row])

    def columns(part):
        return jnp.concatenate([parts[row, :, part, r, :] for r in range(pixel_rows)], axis=1)

    grad_re, grad_im = columns(0), columns(1)
    probe_re, probe_im = own_probe[0], own_probe[1]
    stack = jnp.concatenate([probe_re, grad_re, probe_im, grad_im], axis=0)
    padded = jnp.concatenate([stack, stack, stack, stack], axis=0)
    grams[me] = lax.dot_general(
        stack, padded, (((1,), (1,)), ((), ())), precision=highest_mode, preferred_element_type=jnp.float32
    )

    def gram_copy(other, slot):
        return remote(
            grams.at[me], grams.at[slot], gram_send.at[other], gram_recv.at[slot],
            row=other // 2, col=lax.rem(other, 2),
        )

    def send_gram(step, carry):
        gram_copy(lax.rem(me + step, devices), me).start()
        return carry

    lax.fori_loop(1, devices, send_gram, 0)

    def take_top(k):
        up(k).wait_recv()
        folded[k, :, :half] = folded[k, :, :half] + from_row[k, 0]

    def take_low(k):
        down(k).wait_recv()
        folded[k, :, tall - half :] = folded[k, :, tall - half :] + from_row[k, 1]

    def take_rows(k):
        pl.when(has_down)(lambda: take_top(k))
        pl.when(has_up)(lambda: take_low(k))

    for k in reversed(range(1, layers)):
        take_rows(k)

    def wait_gram(step, carry):
        other = lax.rem(me + step, devices)
        gram_copy(other, other).wait_recv()
        return carry

    lax.fori_loop(1, devices, wait_gram, 0)
    total = lax.fori_loop(1, devices, lambda slot, acc: acc + grams[slot], grams[0])
    count = stack.shape[0] // 2
    gram_re = total[:count, :count] + total[count:, count : 2 * count]
    gram_im = total[:count, count : 2 * count] - total[count:, :count]
    out_re, out_im = eliminate(gram_re, gram_im, probe_re, probe_im, grad_re, grad_im, scale_out)
    out[0] = out_re
    out[1] = out_im
    take_rows(0)
    for k in range(layers):
        pl.when(has_up)(lambda k=k: up(k).wait_send())
        pl.when(has_down)(lambda k=k: down(k).wait_send())

    def finish(step, carry):
        part_copy(lax.rem(row + step, rows), row).wait_send()
        return carry

    lax.fori_loop(1, rows, finish, 0)

    def finish_gram(step, carry):
        gram_copy(lax.rem(me + step, devices), me).wait_send()
        return carry

    lax.fori_loop(1, devices, finish_gram, 0)


def per_device(object_slices, probe, taps, measured, positions):
    modes, _, width, _ = probe.shape
    half = width // 2
    layers, two, tall, wide = object_slices.shape
    records = measured.shape[0]
    rows = lax.axis_size("row")
    anchor = jnp.stack([lax.axis_index("row") * tall - half, lax.axis_index("col") * wide - EDGE])
    places = positions - anchor[None, :]
    pixel_rows = width // (2 * rows)
    share = pixel_rows * width
    own_probe = lax.dynamic_slice_in_dim(probe, lax.axis_index(("row", "col")) * pixel_rows, pixel_rows, 2)
    own_probe = own_probe.reshape(modes, 2, share).transpose(1, 0, 2)
    idx = np.arange(width)
    angle = 2.0 * math.pi / width * (idx[:, None] * idx[None, :] % width)
    dft = np.stack([np.cos(angle), -np.sin(angle)]) / math.sqrt(width)

    f32 = jnp.float32
    smem = pl.BlockSpec(memory_space=pltpu.SMEM)
    vmem = pl.BlockSpec(memory_space=pltpu.VMEM)
    sems = pltpu.SemaphoreType.DMA
    ext_shape = (two, tall + EDGE, wide + 2 * EDGE)
    chip_share = (rows, modes, 2, pixel_rows, width)
    folded, new_probe = pl.pallas_call(
        functools.partial(fused_kernel, rows, float(width), 4),
        out_shape=(
            jax.ShapeDtypeStruct(object_slices.shape, f32),
            jax.ShapeDtypeStruct((2, modes, share), f32),
        ),
        in_specs=[smem, smem] + [vmem] * 5,
        out_specs=(vmem, vmem),
        scratch_shapes=[pltpu.VMEM(ext_shape, f32) for _ in range(layers)]
        + [
            pltpu.VMEM((4, 6 * width, 2 * width), jnp.bfloat16),
            pltpu.VMEM((4, 2 * width, 6 * width), jnp.bfloat16),
            pltpu.VMEM((records, layers - 1, modes, 2, width, width), f32),
            pltpu.VMEM((records, modes, 2, width, width), f32),
            pltpu.VMEM((records, layers, 2, width, width), f32),
            pltpu.VMEM((records, layers, 2, width, width), f32),
            pltpu.VMEM((records, width, width), f32),
            pltpu.VMEM(probe.shape, f32),
            pltpu.VMEM((layers,) + ext_shape, f32),
            pltpu.VMEM((2,) + chip_share, f32),
            pltpu.VMEM(chip_share, f32),
            pltpu.VMEM(chip_share, f32),
            pltpu.VMEM(chip_share, f32),
            pltpu.VMEM((layers, two, tall + EDGE, EDGE), f32),
            pltpu.VMEM((layers, 2, two, half, wide), f32),
            pltpu.VMEM((layers, 2, two, half, wide), f32),
            pltpu.VMEM((2 * rows, 4 * modes, 128), f32),
            pltpu.VMEM((records, width, 2 * (tall + EDGE)), jnp.bfloat16),
            pltpu.VMEM((records, 4 * EDGE, width), jnp.bfloat16),
            pltpu.VMEM((records, tall + EDGE, 2 * width), jnp.bfloat16),
            pltpu.VMEM((records * 2 * width, wide + 2 * EDGE), jnp.bfloat16),
        ]
        + [sems((layers,)) for _ in range(10)]
        + [sems, sems]
        + [sems((layers,)) for _ in range(6)]
        + [sems((rows,)), sems((rows,)), sems((2 * rows,)), sems((2 * rows,))],
        compiler_params=pltpu.CompilerParams(
            collective_id=0, has_side_effects=True, vmem_limit_bytes=56 << 20
        ),
        name="fused",
    )(places, taps, object_slices, probe, own_probe, measured, jnp.asarray(dft, f32))
    return (folded, new_probe.transpose(1, 0, 2))


def solution(mesh):
    placed = (
        P(None, None, ("groups", "row"), "col"),
        P("groups", None, None, None),
        P(),
        P(("groups", "row", "col"), None, None),
        P(("groups", "row", "col"), None),
    )
    return jax.shard_map(
        per_device,
        mesh=mesh,
        in_specs=placed,
        out_specs=(P(None, None, ("groups", "row"), "col"), P("groups", None, ("row", "col"))),
        check_vma=False,
    )
```

time: 231 us -> 96.2 us (0.42)
  waiting for transfers between devices: 71.2 us -> 0 us
  blocking collectives: 57.6 us -> 0 us
  Pallas kernels: 40.3 us -> 88.7 us
  starting transfers between devices: 25 us -> 0 us
  between operations: 14.2 us -> 0.66 us
  other arithmetic: 9.58 us -> 0.64 us
  local copies, waits for them, and re-layouts: 12.4 us -> 5.88 us
    psum x1 -> x0, blocking collectives: 57.6 us -> none  [per_device(): gram = lax.psum(gram_of(own_probe, own_grad), ('row', 'col'))]
    reduce_scatter x1 -> x0, waiting for transfers between devices: 48.6 us -> none  [per_device(): lax.psum_scatter(grad_probe.reshape(modes, 2, pixels), ('row', 'col'), sc...]
    pallas_call x2 -> x1, Pallas kernels: 40.3 us -> 88.7 us  [per_device(): pl.pallas_call(functools.partial(fused_kernel, rows, float(width), 4), ou...]
    ppermute x8 -> x0, starting transfers between devices: 24.9 us -> none  [the longest x2 9.93 us: fold_axis(): lax.ppermute(lax.slice_in_dim(grad, half + inner, full, axis=dim), axis, up)]
    ppermute x8 -> x0, waiting for transfers between devices: 22.6 us -> none  [the longest x2 22.6 us: with_halo(): before = lax.ppermute(last, axis, up)]
    slice x4 -> x0, local copies, waits for them, and re-layouts: 6.89 us -> none  [the longest x2 3.97 us: fold_axis(): lax.slice_in_dim(grad, half + inner, full, axis=dim)]
    add x2 -> x0, other arithmetic: 4.66 us -> none  [fold_axis(): return core + jnp.concatenate([before, after], axis=dim)]
    concatenate x1 -> x0, other arithmetic: 3.97 us -> none  [with_halo(): array = jnp.concatenate([before, array, after], axis=dim)]
  transfers between devices with their start and end apart: 9 -> 0, of which waited for: 3 -> 0; matrix products, arithmetic and copies ran while one was open for 4% -> 0% of each run, Pallas kernels for 1% -> 0%
where the time goes in v3:
time: 96.2 us; the launch traced here: 95.8 us
  Pallas kernels  88.7 us (92%)
  local copies, waits for them, and re-layouts  5.88 us (6%)
    pallas_call x1, Pallas kernels, per_device(): pl.pallas_call(functools.partial(fused_kernel, rows, float(width), 4), ou...  88.7 us
    unnamed x4, local copies, waits for them, and re-layouts  4.39 us

profile of v3, /device:TPU:0, one launch (start us, length us, event | category | flops | bytes accessed | tf_op | source)
XLA Modules:
  0.0 95.8 jit_solution(5889620300531010286)
XLA Ops:
  0.6 0.0 copy-start
  0.6 0.1 pad_add_fusion
  0.7 0.6 copy-done
  1.3 0.6 broadcast_subtract_fusion.places
  1.9 0.8 constant_dynamic-slice_fusion
  2.7 0.7 copy.11
  3.4 88.7 %fused.1 = (f32[4,2,128,256]{3,2,1,0:T(8,128)}, f32[2,8,1024]{2,1,0:T(8,128)}) custom-call(s32[2,2]{1,0:T(2,128)} %broadcast_subtract_fusion.places, f32[2,63]{1,0:T(2,128)} %taps.1, f32[4,2,128,256]{3,2,1,0:T(8,128)} %obj.1, f32[8,2,128,128]{3,2,1,0:T(8,128)} %probe.1, f32[2,8,1024]{2,1,0:T(8,128)} %bitcast.8, f32[2,128,128]{2,1,0:T(8,128)} %measured.1, ...), custom_call_target="tpu_custom_call" | custom-call | tf_op jit(solution)/shard_map/fused/pallas_call | solution.py:494
  92.0 1.5 %copy.9 = f32[8,2,1024]{2,1,0:T(2,128)} copy(f32[8,2,1024]{2,0,1:T(8,128)} %bitcast.9) | data formatting | bytes 131072
  93.6 2.3 %copy.13 = f32[4,2,128,256]{3,2,1,0:T(8,128)} copy(f32[4,2,128,256]{3,2,1,0:T(8,128)} %get-tuple-element.10) | data formatting | bytes 2097152
Async XLA Ops:
  0.6 0.7 copy-start

commit v4 on v3

--- a/solution.py
+++ b/solution.py
@@ -248,8 +248,6 @@
             piece = jnp.dot(pick_rows[rec], piece, preferred_element_type=jnp.float32)
             patch[rec, layer, 0] = piece[:, :width]
             patch[rec, layer, 1] = piece[:, width:]
-        if layer + 1 < layers:
-            pass_halo(layer + 1)
 
         def forward(step, carry, layer=layer):
             base = step * group
@@ -280,7 +278,10 @@
                     level[rec] = level[rec] + total
             return carry
 
-        lax.fori_loop(0, modes // group, forward, 0)
+        forward(0, 0)
+        if layer + 1 < layers:
+            pass_halo(layer + 1)
+        lax.fori_loop(1, modes // group, forward, 0)
 
     level[...] = (2.0 * weight) * (level[...] - measured[...])
     gpatch[...] = jnp.zeros_like(gpatch)
@@ -362,12 +363,13 @@
                     gprobe[base + k, 1] = sums[k][1]
             return carry
 
-        lax.fori_loop(0, modes // group, backward, 0)
+        backward(0, 0)
+        if layer + 1 < layers:
+            send_rows(layer + 1)
+        lax.fori_loop(1, modes // group, backward, 0)
         if layer:
             scatter(layer)
             across(layer).start()
-            if layer + 1 < layers:
-                send_rows(layer + 1)
 
     pixel_rows = chunks.shape[4]
     for chip in range(rows):
@@ -390,7 +392,6 @@
         return carry
 
     lax.fori_loop(1, rows, send_part, 0)
-    send_rows(1)
     send_rows(0)
 
     def take_part(step, total):

time: 96.2 us -> 91.1 us (0.947)
  Pallas kernels: 88.7 us -> 83.6 us
    pallas_call x1, Pallas kernels: 88.7 us -> 83.6 us  [per_device(): pl.pallas_call(functools.partial(fused_kernel, rows, float(width), 4), ou...]
where the time goes in v4:
time: 91.1 us; the launch traced here: 90.8 us
  Pallas kernels  83.6 us (92%)
  local copies, waits for them, and re-layouts  5.88 us (6%)
    pallas_call x1, Pallas kernels, per_device(): pl.pallas_call(functools.partial(fused_kernel, rows, float(width), 4), ou...  83.6 us
    unnamed x4, local copies, waits for them, and re-layouts  4.39 us

profile of v4, /device:TPU:0, one launch (start us, length us, event | category | flops | bytes accessed | tf_op | source)
XLA Modules:
  0.0 90.8 jit_solution(11130727285681799805)
XLA Ops:
  0.6 0.0 copy-start
  0.6 0.1 pad_add_fusion
  0.7 0.6 copy-done
  1.3 0.6 broadcast_subtract_fusion.places
  1.9 0.8 constant_dynamic-slice_fusion
  2.7 0.7 copy.11
  3.4 83.6 %fused.1 = (f32[4,2,128,256]{3,2,1,0:T(8,128)}, f32[2,8,1024]{2,1,0:T(8,128)}) custom-call(s32[2,2]{1,0:T(2,128)} %broadcast_subtract_fusion.places, f32[2,63]{1,0:T(2,128)} %taps.1, f32[4,2,128,256]{3,2,1,0:T(8,128)} %obj.1, f32[8,2,128,128]{3,2,1,0:T(8,128)} %probe.1, f32[2,8,1024]{2,1,0:T(8,128)} %bitcast.8, f32[2,128,128]{2,1,0:T(8,128)} %measured.1, ...), custom_call_target="tpu_custom_call" | custom-call | tf_op jit(solution)/shard_map/fused/pallas_call | solution.py:495
  87.0 1.5 %copy.9 = f32[8,2,1024]{2,1,0:T(2,128)} copy(f32[8,2,1024]{2,0,1:T(8,128)} %bitcast.9) | data formatting | bytes 131072
  88.5 2.3 %copy.13 = f32[4,2,128,256]{3,2,1,0:T(8,128)} copy(f32[4,2,128,256]{3,2,1,0:T(8,128)} %get-tuple-element.10) | data formatting | bytes 2097152
Async XLA Ops:
  0.6 0.7 copy-start
